TPU v7x, 256 devices: a whole 4x4x8 slice. The times are simulated.
256 devices in a mesh: dp: 32 (over x, z), table: 8 (over y, core).
Axes of the slice: x: 4, y: 4, z: 8, core: 2. Of those that a mesh axis runs over, the one named last changes fastest.
Arguments:
- embedding_table: bfloat16 [32768, 512], P('table'), may hold values from -6 to 6
- served_ids: int32 [32, 8, 8, 64], P('dp', 'table'), may hold values from 0 to 4095, as said below
- event_slot: int32 [32, 8, 16, 128], P('dp', 'table'), may hold values from 0 to 511
- block_fill: int32 [32, 8, 16], P('dp', 'table'), may hold values from 0 to 128, as said below
- destination: int32 [32, 8, 16], P('dp', 'table'), may hold values from 0 to 31, as said below
- target: bfloat16 [32, 8, 16, 128, 512], P('dp', 'table'), may hold values from -1.5 to 1.5
- w_in: bfloat16 [512, 1536], replicated, may hold values from -0.25 to 0.25
- w_out: bfloat16 [512, 512], replicated, may hold values from -0.25 to 0.25
- gain_in: float32 [512], replicated, may hold values from 0.1 to 1.9
- gain_out: float32 [512], replicated, may hold values from 0.1 to 1.9
Outputs:
- block_summary: bfloat16 [32, 8, 8, 512], P('dp', 'table')
- row_gradient: float32 [8, 4096, 512], P('table', 'dp')
Inputs may be any that keep to these rules, and one draw needn't show every extreme that they name: `served_ids`: the 64 rows that one owner serves one requester are distinct, and exactly 2 of them lie in each of the 32 runs of 128 consecutive rows. `block_fill`: on each device the blocks with positive fill come first; in every table index some device has all 16 slots live and some device has none. Over blocks with positive fill: one device sends at most 1 block to one destination, reached in every draw, and each device receives exactly 8 blocks in all from the devices of its table index.
All inputs are finite; a program needn't handle non-finite values.
Results may differ from a plain program's by a relative error of at most 0.02.
Values may be sent and summed in bfloat16 or wider, within the bound.
A program may use at most 128 MiB of HBM per device.

v0:
```python
import jax
import jax.numpy as jnp
from jax import lax
from jax.sharding import PartitionSpec as P

H = 4
QK = 64


epsilon = 1e-05


def shortened(value):
    return jax.tree.map(lambda a: a.astype(jnp.bfloat16) if a.dtype == jnp.float32 else a, value)


def layer_norm(values, gain_vector):
    centre = jnp.mean(values, axis=-1, keepdims=True)
    shifted = values - centre
    spread = jnp.mean(shifted * shifted, axis=-1, keepdims=True)
    return shifted * lax.rsqrt(spread + epsilon) * gain_vector


def block_layer(inputs, fill_counts, w_in, w_out, gain_in, gain_out):
    block_count, block_len, feature_dim = inputs.shape
    query_width = H * QK
    values = inputs.astype(jnp.float32)
    normed = layer_norm(values, gain_in).astype(jnp.bfloat16)
    projected = jax.nn.silu(
        jnp.einsum("bed,df->bef", normed, w_in, preferred_element_type=jnp.float32)
    )
    gate_part = projected[..., :feature_dim]
    value_part = (
        projected[..., feature_dim : 2 * feature_dim]
        .astype(jnp.bfloat16)
        .reshape(block_count, block_len, H, feature_dim // H)
    )
    query_part = (
        projected[..., 2 * feature_dim : 2 * feature_dim + query_width]
        .astype(jnp.bfloat16)
        .reshape(block_count, block_len, H, QK)
    )
    key_part = (
        projected[..., 2 * feature_dim + query_width :]
        .astype(jnp.bfloat16)
        .reshape(block_count, block_len, H, QK)
    )
    scores = jnp.einsum(
        "bqhc,bkhc->bhqk", query_part, key_part, preferred_element_type=jnp.float32
    ) * QK ** (-0.5)
    position = jnp.arange(block_len)
    allowed = (position[:, None] >= position[None, :])[None, :, :] & (
        position[None, None, :] < fill_counts[:, None, None]
    )
    attention = jnp.where(allowed[:, None, :, :], jax.nn.silu(scores) / block_len, 0.0).astype(
        jnp.bfloat16
    )
    attended = jnp.einsum(
        "bhqk,bkhc->bqhc", attention, value_part, preferred_element_type=jnp.float32
    ).reshape(block_count, block_len, feature_dim)
    gated_rows = (layer_norm(attended, gain_out) * gate_part).astype(jnp.bfloat16)
    return values + jnp.einsum("bed,df->bef", gated_rows, w_out, preferred_element_type=jnp.float32)


def block_grads(inputs, fill_counts, aims, w_in, w_out, gain_in, gain_out):
    block_len = inputs.shape[1]
    position = jnp.arange(block_len)
    live_mask = (position[None, :] < fill_counts[:, None]).astype(jnp.float32)

    def loss_of(values_in):
        outputs = block_layer(values_in, fill_counts, w_in, w_out, gain_in, gain_out)
        return (jnp.sum(outputs * aims.astype(jnp.float32) * live_mask[:, :, None]), outputs)

    loss_value, pullback, outputs = jax.vjp(loss_of, inputs, has_aux=True)
    input_grads = pullback(jnp.ones_like(loss_value))[0]
    chosen = (position[None, :] == fill_counts[:, None] - 1).astype(jnp.float32)
    summary = jnp.sum(outputs * chosen[:, :, None], axis=1).astype(jnp.bfloat16)
    return (summary, input_grads)


def bucket_plan(fill_counts, destinations, dest_count, capacity):
    live_blocks = fill_counts > 0
    onehot = (
        (destinations[:, None] == jnp.arange(dest_count)[None, :]) & live_blocks[:, None]
    ).astype(jnp.int32)
    earlier = jnp.sum((jnp.cumsum(onehot, axis=0) - onehot) * onehot, axis=1)
    bucket = jnp.where(live_blocks, destinations * capacity + earlier, -1)
    matches = bucket[None, :] == jnp.arange(dest_count * capacity)[:, None]
    source_block = jnp.sum(matches * jnp.arange(fill_counts.shape[0])[None, :], axis=1)
    present = jnp.any(matches, axis=1)
    return (bucket, source_block, present)


def compact_plan(arrived_fill, block_count):
    arrived_live = arrived_fill > 0
    order = jnp.cumsum(arrived_live.astype(jnp.int32)) - 1
    matches = arrived_live[None, :] & (order[None, :] == jnp.arange(block_count)[:, None])
    compact_source = jnp.sum(matches * jnp.arange(arrived_fill.shape[0])[None, :], axis=1)
    return (arrived_live, order, compact_source, jnp.any(matches, axis=1))


def body(
    embedding_table,
    served_ids,
    event_slot,
    block_fill,
    destination,
    target,
    w_in,
    w_out,
    gain_in,
    gain_out,
):
    shard_rows, feature_dim = embedding_table.shape
    dp_count = lax.axis_size("dp")
    owner_ids = served_ids[0, 0]
    table_count, request_cap = owner_ids.shape
    fetched = jnp.take(embedding_table, owner_ids.reshape(-1), axis=0).reshape(
        table_count, request_cap, feature_dim
    )
    arrived = lax.all_to_all(fetched, "table", split_axis=0, concat_axis=0, tiled=True)
    unique_count = table_count * request_cap
    unique_rows = arrived.reshape(unique_count, feature_dim)
    slot_index = event_slot[0, 0]
    block_count, block_len = slot_index.shape
    work_count = block_count // 2
    inputs = jnp.take(unique_rows, slot_index.reshape(-1), axis=0).reshape(
        block_count, block_len, feature_dim
    )
    fill_counts = block_fill[0, 0]
    aims = target[0, 0]
    capacity = max(1, block_count // dp_count)
    slot_total = dp_count * capacity
    bucket, source_block, present = bucket_plan(fill_counts, destination[0, 0], dp_count, capacity)
    bucket_fill = jnp.where(present, jnp.take(fill_counts, source_block), 0).reshape(
        dp_count, capacity
    )
    bucket_inputs = jnp.take(inputs, source_block, axis=0).reshape(
        dp_count, capacity, block_len, feature_dim
    )
    bucket_aims = jnp.take(aims, source_block, axis=0).reshape(
        dp_count, capacity, block_len, feature_dim
    )
    got_inputs, got_aims, got_fill = (
        lax.all_to_all(bucket_inputs, "dp", split_axis=0, concat_axis=0, tiled=True),
        lax.all_to_all(bucket_aims, "dp", split_axis=0, concat_axis=0, tiled=True),
        lax.all_to_all(bucket_fill, "dp", split_axis=0, concat_axis=0, tiled=True),
    )
    arrived_fill = got_fill.reshape(slot_total)
    arrived_live, order, compact_source, compact_present = compact_plan(arrived_fill, work_count)
    work_inputs = jnp.take(
        got_inputs.reshape(slot_total, block_len, feature_dim), compact_source, axis=0
    )
    work_aims = jnp.take(
        got_aims.reshape(slot_total, block_len, feature_dim), compact_source, axis=0
    )
    work_fill = jnp.where(compact_present, jnp.take(arrived_fill, compact_source), 0)
    summary, work_grads = block_grads(
        work_inputs, work_fill, work_aims, w_in, w_out, gain_in, gain_out
    )
    returned = jnp.take(work_grads, jnp.clip(order, 0, work_count - 1), axis=0)
    returned = jnp.where(arrived_live[:, None, None], returned, jnp.zeros_like(returned))
    came_back = lax.all_to_all(
        shortened(returned.reshape(dp_count, capacity, block_len, feature_dim)),
        "dp",
        split_axis=0,
        concat_axis=0,
        tiled=True,
    )
    taken = jnp.take(
        came_back.reshape(slot_total, block_len, feature_dim), jnp.maximum(bucket, 0), axis=0
    )
    input_grads = jnp.where((fill_counts > 0)[:, None, None], taken, jnp.zeros_like(taken))
    flat_grads = input_grads.reshape(-1, feature_dim).astype(jnp.float32)
    unique_grads = jax.ops.segment_sum(
        flat_grads, slot_index.reshape(-1), num_segments=unique_count
    ).astype(jnp.bfloat16)
    sent_home = lax.all_to_all(
        unique_grads.reshape(table_count, request_cap, feature_dim),
        "table",
        split_axis=0,
        concat_axis=0,
        tiled=True,
    )
    owner_total = jax.ops.segment_sum(
        sent_home.reshape(-1, feature_dim).astype(jnp.float32),
        owner_ids.reshape(-1),
        num_segments=shard_rows,
    )
    own_rows = lax.psum_scatter(
        owner_total.astype(jnp.bfloat16), "dp", scatter_dimension=0, tiled=True
    ).astype(jnp.float32)
    return (summary.reshape(1, 1, work_count, feature_dim), own_rows.reshape(1, -1, feature_dim))


def solution(mesh):
    return jax.shard_map(
        body,
        mesh=mesh,
        in_specs=(
            P("table", None),
            P("dp", "table", None, None),
            P("dp", "table", None, None),
            P("dp", "table", None),
            P("dp", "table", None),
            P("dp", "table", None, None, None),
            P(),
            P(),
            P(),
            P(),
        ),
        out_specs=(P("dp", "table", None, None), P("table", "dp", None)),
        check_vma=False,
    )
```

profile of v0, /device:TPU:1, one launch (start us, length us, event | category | flops | bytes accessed | tf_op | source)
XLA Modules:
  0.0 698.2 jit_solution(6052770577938644675)
XLA Ops:
  8.8 4.7 gather_fusion
  14.5 6.6 all-to-all-start
  26.1 4.6 all-to-all-done
  30.6 10.4 %all-to-all-start.2 = ((s32[32,1,1]{2,1,0:T(1,128)}), s32[32,1,1]{2,1,0:T(1,128)S(1)}, u32[]{:S(2)}, u32[]{:S(2)}) async-start(s32[32,1,1]{2,1,0:T(1,128)} %copy.79), calls=%async_computation.2 | async-start | bytes 32768 | tf_op jit(solution)/shard_map/all_to_all | solution.py:147
  41.0 9.2 %gather_fusion.1 = bf16[2048,512]{1,0:T(8,128)(2,1)} fusion(bf16[512,512]{1,0:T(8,128)(2,1)S(1)} %bitcast.156, s32[2048]{0:T(1024)S(1)} %broadcast_clamp_fusion), kind=kCustom, calls=%fused_computation.5 | custom fusion | bytes 4202496 | tf_op jit(solution)/shard_map/jit(_take)/gather | solution.py:127
  54.7 5.9 select_bitcast_fusion
  60.7 101.3 %all_to_all.31 = bf16[32,1,128,512]{3,2,1,0:T(8,128)(2,1)} all-to-all(bf16[32,1,128,512]{3,2,1,0:T(8,128)(2,1)} %get-tuple-element.21), channel_id=1, replica_groups=mesh['dp'=32,'table'=8] {'dp'}, dimensions={0} | all-to-all | bytes 8388608 | tf_op jit(solution)/shard_map/all_to_all | solution.py:146
  162.0 9.0 %all-to-all-start.1 = ((bf16[32,1,128,512]{3,2,1,0:T(8,128)(2,1)}), bf16[32,1,128,512]{3,2,1,0:T(8,128)(2,1)}, u32[]{:S(2)}, u32[]{:S(2)}) async-start(bf16[32,1,128,512]{3,2,1,0:T(8,128)(2,1)} %get-tuple-element.22), calls=%async_computation.1 | async-start | bytes 8388608 | tf_op jit(solution)/shard_map/all_to_all | solution.py:145
  173.1 3.8 gather_fusion.9
  176.9 87.0 %all-to-all-done.1 = bf16[32,1,128,512]{3,2,1,0:T(8,128)(2,1)} async-done(((bf16[32,1,128,512]{3,2,1,0:T(8,128)(2,1)}), bf16[32,1,128,512]{3,2,1,0:T(8,128)(2,1)}, u32[]{:S(2)}, u32[]{:S(2)}) %all-to-all-start.1) | async-done | bytes 4194336 | tf_op jit(solution)/shard_map/all_to_all | solution.py:145
  267.8 5.9 fusion.89
  283.7 3.9 multiply_reduce_fusion
  296.5 3.5 fusion.37
  308.9 7.1 %fusion.32 = (f32[8,128]{1,0:T(8,128)S(1)}, bf16[8,128,512]{2,1,0:T(8,128)(2,1)S(1)}) fusion(f32[512]{0:T(512)S(1)} %copy-done.19, f32[8,128]{1,0:T(8,128)S(1)} %broadcast_multiply_fusion.1, bf16[8,128,512]{2,1,0:T(8,128)(2,1)S(1)} %gather_fusion.7, pred[8]{0:T(512)(128)(4,1)S(1)} %get-tuple-element.10, bf16[512,1536]{1,0:T(8,128)(2,1)} %param.20, ...), kind=kOutput, calls=%fused_computation.56 | convolution fusion | flops 1638398976 | bytes 14166024 | tf_op jit(solution)/shard_map/transpose(jvp(bed,df->bef))/dot_general | solution.py:30
  321.2 4.7 fusion.15
  325.9 9.1 %all-to-all-start.4 = ((bf16[32,1,128,512]{3,2,1,0:T(8,128)(2,1)}), bf16[32,1,128,512]{3,2,1,0:T(8,128)(2,1)}, u32[]{:S(2)}, u32[]{:S(2)}) async-start(bf16[32,1,128,512]{3,2,1,0:T(8,128)(2,1)} %fusion.15), calls=%async_computation.4 | async-start | bytes 8388608 | tf_op jit(solution)/shard_map/all_to_all | solution.py:163
  335.1 93.7 %all-to-all-done.4 = bf16[32,1,128,512]{3,2,1,0:T(8,128)(2,1)} async-done(((bf16[32,1,128,512]{3,2,1,0:T(8,128)(2,1)}), bf16[32,1,128,512]{3,2,1,0:T(8,128)(2,1)}, u32[]{:S(2)}, u32[]{:S(2)}) %all-to-all-start.4) | async-done | bytes 4194336 | tf_op jit(solution)/shard_map/all_to_all | solution.py:163
  434.4 13.6 %scatter_custom_fusion = f32[512,512]{1,0:T(8,128)S(1)} fusion(s32[2048]{0:T(1024)S(1)} %bitcast.173, bf16[2048,512]{1,0:T(8,128)(2,1)} %fusion.38, f32[]{:T(128)} %constant.151.clone.1), kind=kCustom, calls=%fused_computation.32 | custom fusion | flops 2097152 | bytes 3145732 | tf_op jit(solution)/shard_map/scatter-add | solution.py:175
  448.9 7.6 %all-to-all-start.5 = ((bf16[8,64,512]{2,1,0:T(8,128)(2,1)}), bf16[8,64,512]{2,1,0:T(8,128)(2,1)S(1)}, u32[]{:S(2)}, u32[]{:S(2)}) async-start(bf16[8,64,512]{2,1,0:T(8,128)(2,1)} %bitcast.50), calls=%async_computation.5 | async-start | bytes 1048576 | tf_op jit(solution)/shard_map/all_to_all | solution.py:178
  456.6 9.4 %all-to-all-done.5 = bf16[8,64,512]{2,1,0:T(8,128)(2,1)S(1)} async-done(((bf16[8,64,512]{2,1,0:T(8,128)(2,1)}), bf16[8,64,512]{2,1,0:T(8,128)(2,1)S(1)}, u32[]{:S(2)}, u32[]{:S(2)}) %all-to-all-start.5) | async-done | bytes 524320 | tf_op jit(solution)/shard_map/all_to_all | solution.py:178
  466.0 7.4 %scatter_custom_fusion.1 = f32[4096,512]{1,0:T(8,128)} fusion(s32[512]{0:T(512)S(1)} %reshape.644, f32[]{:T(128)} %constant.151.clone.1, bf16[512,512]{1,0:T(8,128)(2,1)S(1)} %bitcast.166), kind=kCustom, calls=%fused_computation.34 | custom fusion | flops 524288 | bytes 8912900 | tf_op jit(solution)/shard_map/scatter-add | solution.py:185
  473.3 5.9 convert_element_type.165
  479.3 4.0 fusion.34
  483.3 206.4 %reduce-scatter.2.cloned.1.call-done = bf16[128,512]{1,0:T(8,128)(2,1)} async-done(((bf16[4096,512]{1,0:T(8,128)(2,1)}), bf16[128,512]{1,0:T(8,128)(2,1)}) %reduce-scatter.2.cloned.1.call-update) | async-done | bytes 131088 | tf_op jit(solution)/shard_map/reduce_scatter | solution.py:190
  (131 shorter events, 59.1 us)
Async XLA Ops:
  7.2 16.2 %copy-start = (bf16[1,1,16,128,512]{4,3,2,1,0:T(8,128)(2,1)S(1)}, bf16[1,1,16,128,512]{4,3,2,1,0:T(8,128)(2,1)}, u32[]{:S(2)}) copy-start(bf16[1,1,16,128,512]{4,3,2,1,0:T(8,128)(2,1)} %param.19) | copy-start | bytes 6291460
  13.5 7.6 %copy-start.2 = (s32[1,1,16]{2,1,0:T(1,128)S(1)}, s32[1,1,16]{2,1,0:T(1,128)}, u32[]{:S(2)}) copy-start(s32[1,1,16]{2,1,0:T(1,128)} %param.17) | copy-start | bytes 196
  13.5 7.6 %copy-start.18 = (s32[1,1,16]{2,1,0:T(1,128)S(1)}, s32[1,1,16]{2,1,0:T(1,128)}, u32[]{:S(2)}) copy-start(s32[1,1,16]{2,1,0:T(1,128)} %param.18) | copy-start | bytes 196
  13.5 8.1 %copy-start.17 = (s32[1,1,16,128]{3,2,1,0:T(8,128)S(1)}, s32[1,1,16,128]{3,2,1,0:T(8,128)}, u32[]{:S(2)}) copy-start(s32[1,1,16,128]{3,2,1,0:T(8,128)} %param.16) | copy-start | bytes 24580
  14.5 16.1 %all-to-all-start = ((bf16[8,64,512]{2,1,0:T(8,128)(2,1)}), bf16[8,64,512]{2,1,0:T(8,128)(2,1)S(1)}, u32[]{:S(2)}, u32[]{:S(2)}) async-start(bf16[8,64,512]{2,1,0:T(8,128)(2,1)} %broadcast_select_fusion.3), calls=%async_computation | async-start | bytes 1048576 | tf_op jit(solution)/shard_map/all_to_all | solution.py:121
  30.6 30.1 %all-to-all-start.2 = ((s32[32,1,1]{2,1,0:T(1,128)}), s32[32,1,1]{2,1,0:T(1,128)S(1)}, u32[]{:S(2)}, u32[]{:S(2)}) async-start(s32[32,1,1]{2,1,0:T(1,128)} %copy.79), calls=%async_computation.2 | async-start | bytes 32768 | tf_op jit(solution)/shard_map/all_to_all | solution.py:147
  162.0 101.9 %all-to-all-start.1 = ((bf16[32,1,128,512]{3,2,1,0:T(8,128)(2,1)}), bf16[32,1,128,512]{3,2,1,0:T(8,128)(2,1)}, u32[]{:S(2)}, u32[]{:S(2)}) async-start(bf16[32,1,128,512]{3,2,1,0:T(8,128)(2,1)} %get-tuple-element.22), calls=%async_computation.1 | async-start | bytes 8388608 | tf_op jit(solution)/shard_map/all_to_all | solution.py:145
  263.9 3.8 copy-start.19
  263.9 3.9 copy-start.21
  273.7 1.6 copy-start.15
  277.2 3.2 copy-start.10
  280.4 1.3 copy-start.4
  281.7 2.0 copy-start.20
  283.7 7.3 %copy-start.3 = (f32[8,128,512]{2,1,0:T(8,128)}, f32[8,128,512]{2,1,0:T(8,128)S(1)}, u32[]{:S(2)}) copy-start(f32[8,128,512]{2,1,0:T(8,128)S(1)} %copy.94) | copy-start | bytes 6291460
  296.5 3.5 copy-start.11
  300.0 3.3 copy-start.6
  303.2 1.6 copy-start.8
  306.1 1.6 copy-start.13
  306.1 2.6 copy-start.12
  325.9 102.9 %all-to-all-start.4 = ((bf16[32,1,128,512]{3,2,1,0:T(8,128)(2,1)}), bf16[32,1,128,512]{3,2,1,0:T(8,128)(2,1)}, u32[]{:S(2)}, u32[]{:S(2)}) async-start(bf16[32,1,128,512]{3,2,1,0:T(8,128)(2,1)} %fusion.15), calls=%async_computation.4 | async-start | bytes 8388608 | tf_op jit(solution)/shard_map/all_to_all | solution.py:163
  448.0 8.5 %copy-start.16 = (s32[1,1,8,64]{3,2,1,0:T(8,128)S(1)}, s32[1,1,8,64]{3,2,1,0:T(8,128)}, u32[]{:S(2)}) copy-start(s32[1,1,8,64]{3,2,1,0:T(8,128)} %param.15) | copy-start | bytes 6148
  448.9 17.1 %all-to-all-start.5 = ((bf16[8,64,512]{2,1,0:T(8,128)(2,1)}), bf16[8,64,512]{2,1,0:T(8,128)(2,1)S(1)}, u32[]{:S(2)}, u32[]{:S(2)}) async-start(bf16[8,64,512]{2,1,0:T(8,128)(2,1)} %bitcast.50), calls=%async_computation.5 | async-start | bytes 1048576 | tf_op jit(solution)/shard_map/all_to_all | solution.py:178
  456.5 233.2 %reduce-scatter.2.cloned.1.call-start = ((), (), s32[]{:S(2)}) async-start(), calls=%async_computation.7 | async-start | bytes 4325376 | tf_op jit(solution)/shard_map/reduce_scatter | solution.py:190
  479.2 212.1 %copy-start.1 = (bf16[1,1,16,128,512]{4,3,2,1,0:T(8,128)(2,1)S(1)}, bf16[1,1,16,128,512]{4,3,2,1,0:T(8,128)(2,1)}, u32[]{:S(2)}) copy-start(bf16[1,1,16,128,512]{4,3,2,1,0:T(8,128)(2,1)} %param.19) | copy-start | bytes 6291460
  (4 other events, 3.8 us)
Sparse Core Ops, SparseCore 0:
  479.4 210.2 reduce-scatter.1
where the time goes:
time: 703 us; the launch traced here: 698 us
  waiting for transfers between devices  401 us (57%)
  blocking collectives  101 us (14%)
  other arithmetic  58.1 us (8%)
  local copies, waits for them, and re-layouts  46.5 us (7%)
  starting transfers between devices  42.6 us (6%)
  matrix products  34.1 us (5%)
  between operations  14.5 us (2%)
    reduce_scatter x1, waiting for transfers between devices, body(): lax.psum_scatter(owner_total.astype(jnp.bfloat16), 'dp', scatter_dimensio...  206 us
    all_to_all x1, blocking collectives, body(): lax.all_to_all(bucket_aims, 'dp', split_axis=0, concat_axis=0, tiled=True)  101 us
    all_to_all x1, waiting for transfers between devices, body(): lax.all_to_all(shortened(returned.reshape(dp_count, capacity, block_len,...  93.7 us
    all_to_all x1, waiting for transfers between devices, body(): lax.all_to_all(bucket_inputs, 'dp', split_axis=0, concat_axis=0, tiled=True)  87 us
  transfers between devices with their start and end apart: 6, of which 5 were waited for; matrix products, arithmetic and copies ran while one was open for 5% of the time, Pallas kernels for 0%

commit v1 on v0

v1 whole, which is shorter than its diff:
```python
import functools

import jax
import jax.numpy as jnp
from jax import lax
from jax.experimental import pallas as pl
from jax.experimental.pallas import tpu as pltpu
from jax.sharding import PartitionSpec as P

H = 4
QK = 64
PACK = 16
LANES = 128
EPS = 1e-05
F32 = jnp.float32
BF16 = jnp.bfloat16
VMEM_BYTES = 48 * 1024 * 1024


def dot(a, b, ca=1, cb=0):
    return lax.dot_general(a, b, (((ca,), (cb,)), ((), ())), preferred_element_type=F32)


def iota(shape, axis):
    return lax.broadcasted_iota(jnp.int32, shape, axis)


def onehot(condition):
    return jnp.where(condition, 1.0, 0.0).astype(BF16)


def sigmoid(x):
    return 0.5 * jnp.tanh(0.5 * x) + 0.5


def column_of(row):
    n = row.shape[1]
    here = iota((n, n), 0) == iota((n, n), 1)
    return jnp.sum(jnp.where(here, row, 0.0), axis=1, keepdims=True)


def fill_order(ids_ref, order_ref, local_ref, run):
    table_count, cap = ids_ref.shape
    unique = table_count * cap
    for t in range(table_count):
        row = ids_ref[t : t + 1, :].astype(F32)
        column = column_of(row)
        rank = jnp.sum(jnp.where(row < column, 1.0, 0.0), axis=1, keepdims=True).astype(jnp.int32)
        place = (rank // 2) * (2 * table_count) + 2 * t + rank % 2
        order_ref[t * cap : (t + 1) * cap, :] = onehot(iota((cap, unique), 1) == place)
        if local_ref is not None:
            local = column.astype(jnp.int32) % run
            local_ref[t * cap : (t + 1) * cap, :] = jnp.broadcast_to(
                local.astype(F32), (cap, run)
            ).astype(BF16)


def greet(dp_count, table_count):
    barrier = pltpu.get_barrier_semaphore()
    me_d, me_t = lax.axis_index("dp"), lax.axis_index("table")

    def signal_dp(step, carry):
        pl.semaphore_signal(barrier, inc=1, device_id={"dp": (me_d + step) % dp_count})
        return carry

    lax.fori_loop(1, dp_count, signal_dp, 0)
    for step in range(1, table_count):
        pl.semaphore_signal(barrier, inc=1, device_id={"table": (me_t + step) % table_count})
    pl.semaphore_wait(barrier, dp_count + table_count - 2)


class Exchange:
    def __init__(self, axis, count, source, target, block, send, recv):
        self.axis, self.count, self.block = axis, count, block
        self.source, self.target, self.send, self.recv = source, target, send, recv
        self.me = lax.axis_index(axis)

    def rows(self, index):
        return pl.ds(pl.multiple_of(index * self.block, self.block), self.block)

    def copy(self, peer, slot):
        return pltpu.make_async_remote_copy(
            src_ref=self.source.at[self.rows(peer)],
            dst_ref=self.target.at[self.rows(slot)],
            send_sem=self.send.at[peer],
            recv_sem=self.recv.at[slot],
            device_id={self.axis: peer},
        )

    def loop(self, step_fn):
        def step(index, carry):
            step_fn((self.me + index) % self.count)
            return carry

        lax.fori_loop(1, self.count, step, 0)

    def start(self):
        self.loop(lambda peer: self.copy(peer, self.me).start())
        self.target[self.rows(self.me), :] = self.source[self.rows(self.me), :]

    def wait_recv(self):
        self.loop(lambda peer: self.copy(peer, peer).wait_recv())

    def wait_send(self):
        self.loop(lambda peer: self.copy(peer, self.me).wait_send())


def fetch_kernel(
    dp_count, ids_ref, table_ref, rows_ref, picks_ref,
    table_v, order, local, picks, sorted_rows, served,
    load_sem, send_t, recv_t, send_d, recv_d,
):
    table_count, cap = ids_ref.shape
    shard_rows, width = table_ref.shape
    unique = table_count * cap
    run = shard_rows // dp_count
    group = min(8, dp_count)
    span, part = group * run, group * 2 * table_count
    loads = []
    for g in range(dp_count // group):
        load = pltpu.make_async_copy(
            table_ref.at[pl.ds(g * span, span)], table_v.at[pl.ds(g * span, span)], load_sem.at[g]
        )
        load.start()
        loads.append(load)
    fill_order(ids_ref, order, local, run)
    index = dot(order[...], local[...], 0, 0)
    picks[...] = onehot(index.astype(jnp.int32) == iota((unique, run), 1))
    greet(dp_count, table_count)
    pick_exchange = Exchange("dp", dp_count, picks, picks_ref, 2 * table_count, send_d, recv_d)
    pick_exchange.start()
    for g, load in enumerate(loads):
        mine = picks[g * part : (g + 1) * part, :]
        wide = jnp.concatenate([mine] * group, axis=1)
        same = iota((part, span), 0) // (2 * table_count) == iota((part, span), 1) // run
        load.wait()
        sorted_rows[g * part : (g + 1) * part, :] = dot(
            jnp.where(same, wide, jnp.zeros_like(wide)), table_v[g * span : (g + 1) * span, :]
        ).astype(BF16)
    served[...] = dot(order[...], sorted_rows[...]).astype(BF16)
    row_exchange = Exchange("table", table_count, served, rows_ref, cap, send_t, recv_t)
    row_exchange.start()
    row_exchange.wait_recv()
    pick_exchange.wait_recv()
    row_exchange.wait_send()
    pick_exchange.wait_send()


def compute_kernel(
    fill_ref, rows_ref, slot_ref, fills_ref, dest_ref, aims_ref, w_in_ref, w_out_ref,
    gain_in_ref, gain_out_ref, grads_ref, message_ref,
    proj, slope, hat, inv, tall, spread, dproj, last,
):
    unique, width = rows_ref.shape
    block_count, length = slot_ref.shape
    query = H * QK
    cols = 2 * width + 2 * query
    head = width // H
    gain_in = gain_in_ref[...]
    gain_out = gain_out_ref[...]

    chunk = min(128, unique)

    def project(i, carry):
        rows = pl.ds(pl.multiple_of(i * chunk, chunk), chunk)
        x = rows_ref[rows, :].astype(F32)
        shifted = x - jnp.mean(x, axis=1, keepdims=True)
        scale = lax.rsqrt(jnp.mean(shifted * shifted, axis=1, keepdims=True) + EPS)
        normal = shifted * scale
        hat[rows, :] = normal
        inv[rows, :] = jnp.broadcast_to(scale, (chunk, LANES))
        normed = (normal * gain_in).astype(BF16)
        for c in range(0, cols, width):
            pre = dot(normed, w_in_ref[:, c : c + width])
            sig = sigmoid(pre)
            act = pre * sig
            proj[rows, c : c + width] = act.astype(BF16)
            slope[rows, c : c + width] = sig + act * (1.0 - sig)
        return carry

    lax.fori_loop(0, unique // chunk, project, 0)

    causal = iota((length, length), 0) >= iota((length, length), 1)
    key_lane = iota((length, length), 1)
    query_head = iota((length, query), 1) // QK
    position = iota((length, 1), 0)
    slots = slot_ref[...].astype(F32)
    eye = iota((length, length), 0) == iota((length, length), 1)

    def one_block(b):
        rows = pl.ds(pl.multiple_of(b * length, length), length)
        fill = fill_ref[b]
        slot_row = slot_ref[pl.ds(b, 1), :].astype(F32)
        slot_col = jnp.sum(jnp.where(eye, slot_row, 0.0), axis=1, keepdims=True).astype(jnp.int32)
        here = onehot(iota((length, unique), 1) == slot_col)
        aim = aims_ref[rows, :]
        live_aim = jnp.where(position < fill, aim, jnp.zeros_like(aim))
        spread[rows, cols:] = live_aim
        dgated = dot(live_aim, w_out_ref[...], 1, 1)
        gate = dot(here, proj[:, :width])
        value = dot(here, proj[:, width : 2 * width]).astype(BF16)
        qk = dot(here, proj[:, 2 * width :]).astype(BF16)
        q, k = qk[:, :query], qk[:, query:]
        zero = jnp.zeros_like(q)
        q4 = jnp.concatenate([jnp.where(query_head == h, q, zero) for h in range(H)], axis=0)
        k4 = jnp.concatenate([jnp.where(query_head == h, k, zero) for h in range(H)], axis=0)
        raw = dot(q4, k, 1, 1)
        seen = causal & (key_lane < fill)
        weights, slopes, attended = [], [], []
        for h in range(H):
            s = raw[h * length : (h + 1) * length, :] * QK ** (-0.5)
            sig = sigmoid(s)
            act = s * sig
            weight = jnp.where(seen, act * (1.0 / length), 0.0).astype(BF16)
            weights.append(weight)
            slopes.append(
                jnp.where(seen, (sig + act * (1.0 - sig)) * (QK ** (-0.5) / length), 0.0)
            )
            attended.append(dot(weight, value[:, h * head : (h + 1) * head]))
        attended = jnp.concatenate(attended, axis=1)
        shifted = attended - jnp.mean(attended, axis=1, keepdims=True)
        scale = lax.rsqrt(jnp.mean(shifted * shifted, axis=1, keepdims=True) + EPS)
        normal = shifted * scale
        out = normal * gain_out
        last[pl.ds(b, 1), :] = jnp.sum(
            jnp.where(position == fill - 1, out * gate, 0.0), axis=0, keepdims=True
        )
        spread[rows, :width] = (dgated * out).astype(BF16)
        dnormal = dgated * gate * gain_out
        dattended = scale * (
            dnormal
            - jnp.mean(dnormal, axis=1, keepdims=True)
            - normal * jnp.mean(dnormal * normal, axis=1, keepdims=True)
        )
        dattended = dattended.astype(BF16)
        dscores = []
        for h in range(H):
            part = slice(h * head, (h + 1) * head)
            dweight = dot(dattended[:, part], value[:, part], 1, 1)
            dscores.append((dweight * slopes[h]).astype(BF16))
            spread[rows, width + h * head : width + (h + 1) * head] = dot(
                weights[h], dattended[:, part], 0, 0
            ).astype(BF16)
        spread[rows, 2 * width : 2 * width + query] = dot(
            jnp.concatenate(dscores, axis=1), k4
        ).astype(BF16)
        spread[rows, 2 * width + query : cols] = dot(
            jnp.concatenate(dscores, axis=0), q4, 0, 0
        ).astype(BF16)

    def pair(i, carry):
        one_block(2 * i)
        one_block(2 * i + 1)
        return carry

    lax.fori_loop(0, block_count // 2, pair, 0)

    tile = min(256, unique)
    for r in range(0, unique, tile):
        rows = slice(r, r + tile)
        for b in range(block_count):
            tall[:, b * length : (b + 1) * length] = onehot(
                iota((tile, length), 0) + r == slot_ref[b : b + 1, :]
            )
        for c in range(0, cols, width):
            total = dot(tall[...], spread[:, c : c + width])
            dproj[:, c : c + width] = (total * slope[rows, c : c + width]).astype(BF16)
        dhat = dot(dproj[...], w_in_ref[...], 1, 1) * gain_in
        normal = hat[rows, :]
        scale = inv[rows, :1]
        dx = scale * (
            dhat
            - jnp.mean(dhat, axis=1, keepdims=True)
            - normal * jnp.mean(dhat * normal, axis=1, keepdims=True)
        )
        grads_ref[rows, :] = (dx + dot(tall[...], spread[:, cols:])).astype(BF16)

    fills = fills_ref[...]
    fill_col = column_of(fills.astype(F32)).astype(jnp.int32)
    last_slot = jnp.sum(
        jnp.where(iota((block_count, length), 1) == fill_col - 1, slots, 0.0),
        axis=1,
        keepdims=True,
    ).astype(jnp.int32)
    last_rows = dot(onehot(iota((block_count, unique), 1) == last_slot), rows_ref[...])
    summary = (last_rows + dot(last[...].astype(BF16), w_out_ref[...])).astype(BF16)
    total_rows = message_ref.shape[0]
    row = iota((total_rows, block_count), 0)
    chosen = (row // PACK == dest_ref[...]) & (fills > 0)
    flag = jnp.sum(jnp.where(chosen & (row % PACK == width // LANES), 1.0, 0.0), axis=1, keepdims=True)
    message = jnp.broadcast_to(flag, message_ref.shape)
    for i in range(width // LANES):
        message = message + dot(
            onehot(chosen & (row % PACK == i)), summary[:, i * LANES : (i + 1) * LANES]
        )
    message_ref[...] = message.astype(BF16)


def return_kernel(
    dp_count, ids_ref, grads_ref, message_ref, picks_ref, summary_ref, total_ref,
    order, home, ordered, arrived, letters,
    send_t, recv_t, send_d, recv_d, send_m, recv_m,
):
    table_count, cap = ids_ref.shape
    unique, width = grads_ref.shape
    greet(dp_count, table_count)
    home_exchange = Exchange("table", table_count, grads_ref, home, cap, send_t, recv_t)
    home_exchange.start()
    letter_exchange = Exchange("dp", dp_count, message_ref, letters, PACK, send_m, recv_m)
    letter_exchange.start()
    fill_order(ids_ref, order, None, picks_ref.shape[1])
    home_exchange.wait_recv()
    ordered[...] = dot(order[...], home[...], 0, 0).astype(BF16)
    total_exchange = Exchange("dp", dp_count, ordered, arrived, 2 * table_count, send_d, recv_d)
    total_exchange.start()
    letter_exchange.wait_recv()
    rows = letters.shape[0]
    row, col = iota((rows, rows), 0), iota((rows, rows), 1)
    flag_col = col % PACK == width // LANES
    rank = dot(onehot(flag_col & (col // PACK < row // PACK)), letters[...])
    present = dot(onehot(flag_col & (col // PACK == row // PACK)), letters[...])
    lane = iota((rows, LANES), 1)
    wanted = (present > 0.5) & (rank.astype(jnp.int32) == lane)
    kind = iota((rows, LANES), 0) % PACK
    work = summary_ref.shape[0]
    for i in range(width // LANES):
        part = dot(onehot(wanted & (kind == i)), letters[...], 0, 0)
        summary_ref[:, i * LANES : (i + 1) * LANES] = part[:work, :].astype(BF16)
    total_exchange.wait_recv()
    total_ref[...] = dot(picks_ref[...], arrived[...], 0, 0)
    home_exchange.wait_send()
    letter_exchange.wait_send()
    total_exchange.wait_send()


def whole(space=pltpu.VMEM):
    return pl.BlockSpec(memory_space=space)


def body(
    embedding_table, served_ids, event_slot, block_fill, destination, target, w_in, w_out,
    gain_in, gain_out,
):
    dp_count, table_count = lax.axis_size("dp"), lax.axis_size("table")
    shard_rows, width = embedding_table.shape
    ids = served_ids[0, 0]
    cap = ids.shape[1]
    unique = table_count * cap
    run = shard_rows // dp_count
    slots = event_slot[0, 0]
    block_count, length = slots.shape
    work_count = block_count // 2
    events = block_count * length
    cols = w_in.shape[1]
    dma = pltpu.SemaphoreType.DMA
    params = functools.partial(pltpu.CompilerParams, vmem_limit_bytes=VMEM_BYTES)
    rows, picks = pl.pallas_call(
        functools.partial(fetch_kernel, dp_count),
        out_shape=(
            jax.ShapeDtypeStruct((unique, width), BF16),
            jax.ShapeDtypeStruct((unique, run), BF16),
        ),
        in_specs=[whole(), whole(pl.ANY)],
        out_specs=(whole(), whole()),
        scratch_shapes=[
            pltpu.VMEM((shard_rows, width), BF16),
            pltpu.VMEM((unique, unique), BF16),
            pltpu.VMEM((unique, run), BF16),
            pltpu.VMEM((unique, run), BF16),
            pltpu.VMEM((unique, width), BF16),
            pltpu.VMEM((unique, width), BF16),
            dma((max(1, dp_count // 8),)),
            dma((table_count,)), dma((table_count,)), dma((dp_count,)), dma((dp_count,)),
        ],
        compiler_params=params(collective_id=0, has_side_effects=True),
        name="fetch",
    )(ids, embedding_table)
    fills = block_fill[0, 0]
    grads, message = pl.pallas_call(
        compute_kernel,
        out_shape=(
            jax.ShapeDtypeStruct((unique, width), BF16),
            jax.ShapeDtypeStruct((dp_count * PACK, LANES), BF16),
        ),
        in_specs=[whole(pltpu.SMEM)] + [whole()] * 9,
        out_specs=(whole(), whole()),
        scratch_shapes=[
            pltpu.VMEM((unique, cols), BF16),
            pltpu.VMEM((unique, cols), F32),
            pltpu.VMEM((unique, width), F32),
            pltpu.VMEM((unique, LANES), F32),
            pltpu.VMEM((min(256, unique), events), BF16),
            pltpu.VMEM((events, cols + width), BF16),
            pltpu.VMEM((min(256, unique), cols), BF16),
            pltpu.VMEM((block_count, width), F32),
        ],
        compiler_params=params(),
        name="compute",
    )(
        fills, rows, slots, fills.reshape(1, -1), destination[0, 0].reshape(1, -1),
        target.reshape(events, width), w_in, w_out, gain_in.reshape(1, -1), gain_out.reshape(1, -1),
    )
    summary, total = pl.pallas_call(
        functools.partial(return_kernel, dp_count),
        out_shape=(
            jax.ShapeDtypeStruct((work_count, width), BF16),
            jax.ShapeDtypeStruct((run, width), F32),
        ),
        in_specs=[whole()] * 4,
        out_specs=(whole(), whole()),
        scratch_shapes=[
            pltpu.VMEM((unique, unique), BF16),
            pltpu.VMEM((unique, width), BF16),
            pltpu.VMEM((unique, width), BF16),
            pltpu.VMEM((unique, width), BF16),
            pltpu.VMEM((dp_count * PACK, LANES), BF16),
            dma((table_count,)), dma((table_count,)), dma((dp_count,)), dma((dp_count,)),
            dma((dp_count,)), dma((dp_count,)),
        ],
        compiler_params=params(collective_id=1, has_side_effects=True),
        name="return_home",
    )(ids, grads, message, picks)
    return (summary.reshape(1, 1, work_count, width), total.reshape(1, run, width))


def solution(mesh):
    return jax.shard_map(
        body,
        mesh=mesh,
        in_specs=(
            P("table", None),
            P("dp", "table", None, None),
            P("dp", "table", None, None),
            P("dp", "table", None),
            P("dp", "table", None),
            P("dp", "table", None, None, None),
            P(), P(), P(), P(),
        ),
        out_specs=(P("dp", "table", None, None), P("table", "dp", None)),
        check_vma=False,
    )
```

time: 703 us -> 92.8 us (0.13)
  waiting for transfers between devices: 401 us -> 0 us
  blocking collectives: 101 us -> 0 us
  Pallas kernels: 0 us -> 87 us
  other arithmetic: 58.1 us -> 0 us
  starting transfers between devices: 42.6 us -> 0 us
  local copies, waits for them, and re-layouts: 46.5 us -> 4.89 us
  matrix products: 34.1 us -> 0 us
  between operations: 14.5 us -> 0.76 us
    reduce_scatter x1 -> x0, waiting for transfers between devices: 206 us -> none  [body(): lax.psum_scatter(owner_total.astype(jnp.bfloat16), 'dp', scatter_dimensio...]
    all_to_all x5 -> x0, waiting for transfers between devices: 195 us -> none  [the longest x1 93.7 us: body(): lax.all_to_all(shortened(returned.reshape(dp_count, capacity, block_len,...]
    all_to_all x1 -> x0, blocking collectives: 101 us -> none  [body(): lax.all_to_all(bucket_aims, 'dp', split_axis=0, concat_axis=0, tiled=True)]
    pallas_call x0 -> x3, Pallas kernels: none -> 87 us  [the longest x1 33.4 us: body(): pl.pallas_call(compute_kernel, out_shape=(jax.ShapeDtypeStruct((unique, w...]
    all_to_all x5 -> x0, starting transfers between devices: 42.6 us -> none  [the longest x1 10.4 us: body(): lax.all_to_all(bucket_fill, 'dp', split_axis=0, concat_axis=0, tiled=True)]
    dot_general x10 -> x0, matrix products: 34.1 us -> none  [the longest x2 13 us: block_layer(): jnp.einsum('bed,df->bef', normed, w_in, preferred_element_type=jnp.float32)]
    gather x10 -> x0, local copies, waits for them, and re-layouts: 33.2 us -> none  [the longest x1 9.18 us: body(): jnp.take(unique_rows, slot_index.reshape(-1), axis=0)]
    scatter-add x2 -> x0, other arithmetic: 20.9 us -> none  [the longest x1 13.6 us: body(): jax.ops.segment_sum(flat_grads, slot_index.reshape(-1), num_segments=uniq...]
  transfers between devices with their start and end apart: 6 -> 0, of which waited for: 5 -> 0; matrix products, arithmetic and copies ran while one was open for 5% -> 0% of each run, Pallas kernels for 0% -> 0%
where the time goes in v1:
time: 92.8 us; the launch traced here: 92.7 us
  Pallas kernels  87 us (94%)
  local copies, waits for them, and re-layouts  4.89 us (5%)
    pallas_call x1, Pallas kernels, body(): pl.pallas_call(compute_kernel, out_shape=(jax.ShapeDtypeStruct((unique, w...  33.4 us
    pallas_call x1, Pallas kernels, body(): pl.pallas_call(functools.partial(return_kernel, dp_count), out_shape=(jax...  29 us
    pallas_call x1, Pallas kernels, body(): pl.pallas_call(functools.partial(fetch_kernel, dp_count), out_shape=(jax....  24.6 us
    unnamed x22, local copies, waits for them, and re-layouts  4.89 us

profile of v1, /device:TPU:1, one launch (start us, length us, event | category | flops | bytes accessed | tf_op | source)
XLA Modules:
  0.0 92.7 jit_solution(5953720238208854179)
XLA Ops:
  0.6 0.0 copy-start
  0.6 2.2 %copy-done = bf16[4096,512]{1,0:T(8,128)(2,1)S(1)} copy-done((bf16[4096,512]{1,0:T(8,128)(2,1)S(1)}, bf16[4096,512]{1,0:T(8,128)(2,1)}, u32[]{:S(2)}) %copy-start) | copy-done | bytes 4194328
  2.8 0.0 copy-start.4
  2.8 0.7 copy-done.4
  3.5 0.0 copy-start.1
  3.5 0.0 copy-start.2
  3.5 0.0 copy-start.3
  3.5 0.0 copy-start.7
  3.5 0.0 copy-start.8
  3.5 0.0 copy-start.9
  3.6 24.6 %fetch.1 = (bf16[512,512]{1,0:T(8,128)(2,1)S(1)}, bf16[512,128]{1,0:T(8,128)(2,1)S(1)}) custom-call(s32[8,64]{1,0:T(8,128)S(1)} %bitcast.12, bf16[4096,512]{1,0:T(8,128)(2,1)S(1)} %copy-done), custom_call_target="tpu_custom_call" | custom-call | tf_op jit(solution)/shard_map/fetch/pallas_call | solution.py:357
  28.2 0.0 copy-done.1
  28.2 0.0 copy-done.2
  28.2 0.0 copy-done.3
  28.2 0.0 copy-done.6
  28.2 0.0 copy-done.7
  28.2 0.0 copy-done.8
  28.2 0.0 copy-done.9
  28.2 0.0 copy-start.5
  28.3 0.7 copy-done.5
  28.9 33.4 %compute.1 = (bf16[512,512]{1,0:T(8,128)(2,1)S(1)}, bf16[512,128]{1,0:T(8,128)(2,1)S(1)}) custom-call(s32[16]{0:T(128)S(1)} %bitcast.18, bf16[512,512]{1,0:T(8,128)(2,1)S(1)} %get-tuple-element.8.rows_ref, s32[16,128]{1,0:T(8,128)S(1)} %bitcast.14, s32[1,16]{1,0:T(1,128)S(1)} %bitcast.19, s32[1,16]{1,0:T(1,128)S(1)} %bitcast.20, ...), custom_call_target="tpu_custom_call" | custom-call | tf_op jit(solution)/shard_map/compute/pallas_call | solution.py:379
  62.4 29.0 %return_home.1 = (bf16[8,512]{1,0:T(8,128)(2,1)S(1)}, f32[128,512]{1,0:T(8,128)S(1)}) custom-call(s32[8,64]{1,0:T(8,128)S(1)} %bitcast.13, bf16[512,512]{1,0:T(8,128)(2,1)S(1)} %get-tuple-element.9.grads_ref, bf16[512,128]{1,0:T(8,128)(2,1)S(1)} %get-tuple-element.10.message_ref, bf16[512,128]{1,0:T(8,128)(2,1)S(1)} %get-tuple-element.11.picks_ref), custom_call_target="tpu_custom_call" | custom-call | tf_op jit(solution)/shard_map/return_home/pallas_call | solution.py:403
  91.3 0.6 copy.14
  91.9 0.7 copy.15
  (1 shorter events, 0.0 us)
Async XLA Ops:
  0.6 2.2 %copy-start = (bf16[4096,512]{1,0:T(8,128)(2,1)S(1)}, bf16[4096,512]{1,0:T(8,128)(2,1)}, u32[]{:S(2)}) copy-start(bf16[4096,512]{1,0:T(8,128)(2,1)} %table_ref.1) | copy-start | bytes 12582916
  2.8 0.7 copy-start.4
  3.5 24.7 %copy-start.1 = (bf16[1,1,16,128,512]{4,3,2,1,0:T(8,128)(2,1)S(1)}, bf16[1,1,16,128,512]{4,3,2,1,0:T(8,128)(2,1)}, u32[]{:S(2)}) copy-start(bf16[1,1,16,128,512]{4,3,2,1,0:T(8,128)(2,1)} %param.15) | copy-start | bytes 6291460
  3.5 24.7 %copy-start.2 = (bf16[512,1536]{1,0:T(8,128)(2,1)S(1)}, bf16[512,1536]{1,0:T(8,128)(2,1)}, u32[]{:S(2)}) copy-start(bf16[512,1536]{1,0:T(8,128)(2,1)} %w_in_ref.1) | copy-start | bytes 4718596
  3.5 24.7 %copy-start.3 = (bf16[512,512]{1,0:T(8,128)(2,1)S(1)}, bf16[512,512]{1,0:T(8,128)(2,1)}, u32[]{:S(2)}) copy-start(bf16[512,512]{1,0:T(8,128)(2,1)} %w_out_ref.1) | copy-start | bytes 1572868
  3.5 24.7 %copy-start.6 = (f32[512]{0:T(512)S(1)}, f32[512]{0:T(512)}, u32[]{:S(2)}) copy-start(f32[512]{0:T(512)} %param.18) | copy-start | bytes 6148
  3.5 24.7 %copy-start.7 = (f32[512]{0:T(512)S(1)}, f32[512]{0:T(512)}, u32[]{:S(2)}) copy-start(f32[512]{0:T(512)} %param.19) | copy-start | bytes 6148
  3.5 24.7 %copy-start.8 = (s32[1,1,16]{2,1,0:T(1,128)S(1)}, s32[1,1,16]{2,1,0:T(1,128)}, u32[]{:S(2)}) copy-start(s32[1,1,16]{2,1,0:T(1,128)} %param.13) | copy-start | bytes 196
  3.5 24.7 %copy-start.9 = (s32[1,1,16]{2,1,0:T(1,128)S(1)}, s32[1,1,16]{2,1,0:T(1,128)}, u32[]{:S(2)}) copy-start(s32[1,1,16]{2,1,0:T(1,128)} %param.14) | copy-start | bytes 196
  28.2 0.7 copy-start.5

commit v2 on v1

v2 whole, which is shorter than its diff:
```python
import functools

import jax
import jax.numpy as jnp
from jax import lax
from jax.experimental import pallas as pl
from jax.experimental.pallas import tpu as pltpu
from jax.sharding import PartitionSpec as P

H = 4
QK = 64
PACK = 16
LANES = 128
EPS = 1e-05
F32 = jnp.float32
BF16 = jnp.bfloat16
VMEM_BYTES = 48 * 1024 * 1024
PROJECT_ROWS = 128
GATHER_ROWS = 256
BLOCK_GROUP = 2
FINISH_ROWS = 256
PARTS = 2


def dot(a, b, ca=1, cb=0):
    return lax.dot_general(a, b, (((ca,), (cb,)), ((), ())), preferred_element_type=F32)


def iota(shape, axis):
    return lax.broadcasted_iota(jnp.int32, shape, axis)


def onehot(condition):
    return jnp.where(condition, 1.0, 0.0).astype(BF16)


def sigmoid(x):
    return 0.5 * jnp.tanh(0.5 * x) + 0.5


def column_of(row):
    n = row.shape[1]
    here = iota((n, n), 0) == iota((n, n), 1)
    return jnp.sum(jnp.where(here, row, 0.0), axis=1, keepdims=True)


def fill_order(ids_ref, order_ref, local_ref, run):
    table_count, cap = ids_ref.shape
    unique = table_count * cap
    for t in range(table_count):
        row = ids_ref[t : t + 1, :].astype(F32)
        column = column_of(row)
        rank = jnp.sum(jnp.where(row < column, 1.0, 0.0), axis=1, keepdims=True).astype(jnp.int32)
        place = (rank // 2) * (2 * table_count) + 2 * t + rank % 2
        order_ref[t * cap : (t + 1) * cap, :] = onehot(iota((cap, unique), 1) == place)
        if local_ref is not None:
            local = column.astype(jnp.int32) % run
            local_ref[t * cap : (t + 1) * cap, :] = jnp.broadcast_to(
                local.astype(F32), (cap, run)
            ).astype(BF16)


def greet(barrier, dp_count, table_count):
    me_d, me_t = lax.axis_index("dp"), lax.axis_index("table")

    def signal_dp(step, carry):
        pl.semaphore_signal(barrier, inc=1, device_id={"dp": (me_d + step) % dp_count})
        return carry

    lax.fori_loop(1, dp_count, signal_dp, 0)
    for step in range(1, table_count):
        pl.semaphore_signal(barrier, inc=1, device_id={"table": (me_t + step) % table_count})


class Exchange:
    def __init__(self, axis, count, source, target, block, sems):
        self.axis, self.count, self.block = axis, count, block
        self.source, self.target = source, target
        self.send, self.recv = sems
        self.me = lax.axis_index(axis)

    def rows(self, index):
        return pl.ds(pl.multiple_of(index * self.block, self.block), self.block)

    def copy(self, peer, slot):
        return pltpu.make_async_remote_copy(
            src_ref=self.source.at[self.rows(peer)],
            dst_ref=self.target.at[self.rows(slot)],
            send_sem=self.send.at[peer],
            recv_sem=self.recv.at[slot],
            device_id={self.axis: peer},
        )

    def loop(self, step_fn):
        def step(index, carry):
            step_fn((self.me + index) % self.count)
            return carry

        lax.fori_loop(1, self.count, step, 0)

    def start(self):
        self.loop(lambda peer: self.copy(peer, self.me).start())
        self.target[self.rows(self.me), :] = self.source[self.rows(self.me), :]

    def wait_recv(self):
        self.loop(lambda peer: self.copy(peer, peer).wait_recv())

    def wait_send(self):
        self.loop(lambda peer: self.copy(peer, self.me).wait_send())


def prepare(fill_ref, slot_ref, w_out_ref, here, tall, spread, dgated):
    block_count, length = slot_ref.shape
    unique = here.shape[1]
    cols = spread.shape[1] - w_out_ref.shape[0]
    eye = iota((length, length), 0) == iota((length, length), 1)
    position = iota((length, 1), 0)

    def one(b, carry):
        rows = pl.ds(pl.multiple_of(b * length, length), length)
        slot_row = slot_ref[pl.ds(b, 1), :]
        slot_col = jnp.sum(
            jnp.where(eye, slot_row.astype(F32), 0.0), axis=1, keepdims=True
        ).astype(jnp.int32)
        here[rows, :] = onehot(iota((length, unique), 1) == slot_col)
        tall[:, rows] = onehot(iota((unique, length), 0) == slot_row)
        aim = spread[rows, cols:]
        live_aim = jnp.where(position < fill_ref[b], aim, jnp.zeros_like(aim))
        spread[rows, cols:] = live_aim
        dgated[rows, :] = dot(live_aim, w_out_ref[...], 1, 1).astype(BF16)
        return carry

    lax.fori_loop(0, block_count, one, 0)


def project(rows_ref, w_in_ref, gain_in_ref, gain_out_ref, length, proj, slope, hat, inv):
    unique, width = rows_ref.shape
    query = H * QK
    gain_in = gain_in_ref[...]
    half = 0.5 * QK ** (-0.5)
    lane = iota((1, 2 * query), 1)
    factors = [gain_out_ref[...], 1.0 / length, jnp.where(lane < query, half, 1.0)]
    chunk = min(PROJECT_ROWS, unique)

    def step(i, carry):
        rows = pl.ds(pl.multiple_of(i * chunk, chunk), chunk)
        x = rows_ref[rows, :].astype(F32)
        shifted = x - jnp.mean(x, axis=1, keepdims=True)
        scale = lax.rsqrt(jnp.mean(shifted * shifted, axis=1, keepdims=True) + EPS)
        normal = shifted * scale
        hat[rows, :] = normal
        inv[rows, :] = jnp.broadcast_to(scale, (chunk, LANES))
        normed = (normal * gain_in).astype(BF16)
        for c, factor in enumerate(factors):
            part = slice(c * width, (c + 1) * width)
            pre = dot(normed, w_in_ref[:, part])
            sig = sigmoid(pre)
            act = pre * sig
            proj[rows, part] = (act * factor).astype(BF16)
            slope[rows, part] = (sig + act * (1.0 - sig)) * factor
        return carry

    lax.fori_loop(0, unique // chunk, step, 0)


def gather(here, proj, spread):
    events = here.shape[0]
    cols = proj.shape[1]
    chunk = min(GATHER_ROWS, events)
    width = cols // 3

    def step(i, carry):
        rows = pl.ds(pl.multiple_of(i * chunk, chunk), chunk)
        for c in range(0, cols, width):
            spread[rows, c : c + width] = dot(here[rows, :], proj[:, c : c + width]).astype(BF16)
        return carry

    lax.fori_loop(0, events // chunk, step, 0)


def attend(fill_ref, length, spread, dgated, normals, last):
    events, width = dgated.shape
    query = H * QK
    cols = 2 * width + 2 * query
    head = width // H
    block_count = events // length
    group = min(BLOCK_GROUP, block_count)
    causal = iota((length, length), 0) >= iota((length, length), 1)
    key_lane = iota((length, length), 1)
    low = iota((length, LANES), 1) < QK

    def heads(x):
        zero = jnp.zeros((length, LANES), BF16)
        parts = []
        for h in range(H):
            side = h // 2
            mine = x[:, side * LANES : (side + 1) * LANES]
            mine = jnp.where(low if h % 2 == 0 else ~low, mine, zero)
            parts.append(jnp.concatenate([mine, zero] if side == 0 else [zero, mine], axis=1))
        return jnp.concatenate(parts, axis=0)

    def step(i, carry):
        blocks = [group * i + n for n in range(group)]
        rows = [pl.ds(pl.multiple_of(b * length, length), length) for b in blocks]
        fills = [fill_ref[b] for b in blocks]
        n_all = range(group)
        q4, k4, half = [], [], []
        for n in n_all:
            q = spread[rows[n], 2 * width : 2 * width + query]
            k = spread[rows[n], 2 * width + query : cols]
            q4.append(heads(q))
            k4.append(heads(k))
            half.append(dot(q4[n], k, 1, 1))
        weights, slopes, attended = [], [], []
        for n in n_all:
            seen = causal & (key_lane < fills[n])
            ws, ss, parts = [], [], []
            for h in range(H):
                s = half[n][h * length : (h + 1) * length, :]
                up = jnp.where(seen, jnp.tanh(s) + 1.0, 0.0)
                act = s * up
                ws.append(act.astype(BF16))
                ss.append(up * ((s - act) + (s + 1.0)))
                value = spread[rows[n], width + h * head : width + (h + 1) * head]
                parts.append(dot(ws[h], value))
            weights.append(ws)
            slopes.append(ss)
            attended.append(jnp.concatenate(parts, axis=1))
        shifted = [a - jnp.mean(a, axis=1, keepdims=True) for a in attended]
        scale = [lax.rsqrt(jnp.mean(a * a, axis=1, keepdims=True) + EPS) for a in shifted]
        dattended = []
        for n in n_all:
            normal = shifted[n] * scale[n]
            normals[n * length : (n + 1) * length, :] = normal
            gate = spread[rows[n], :width].astype(F32)
            upper = dgated[rows[n], :].astype(F32)
            dnormal = upper * gate
            spread[rows[n], :width] = (upper * normal).astype(BF16)
            where = jnp.maximum(fills[n] - 1, 0)
            last[pl.ds(blocks[n], 1), :] = normals[pl.ds(n * length + where, 1), :]
            mean = jnp.mean(dnormal, axis=1, keepdims=True)
            along = jnp.mean(dnormal * normal, axis=1, keepdims=True)
            dattended.append((scale[n] * (dnormal - mean - normal * along)).astype(BF16))
        dscores = []
        for n in n_all:
            ds = []
            for h in range(H):
                part = slice(h * head, (h + 1) * head)
                there = slice(width + h * head, width + (h + 1) * head)
                dweight = dot(dattended[n][:, part], spread[rows[n], there], 1, 1)
                ds.append((dweight * slopes[n][h]).astype(BF16))
                spread[rows[n], there] = dot(weights[n][h], dattended[n][:, part], 0, 0).astype(BF16)
            dscores.append(ds)
        for n in n_all:
            spread[rows[n], 2 * width : 2 * width + query] = dot(
                jnp.concatenate(dscores[n], axis=1), k4[n]
            ).astype(BF16)
            spread[rows[n], 2 * width + query : cols] = dot(
                jnp.concatenate(dscores[n], axis=0), q4[n], 0, 0
            ).astype(BF16)
        return carry

    lax.fori_loop(0, block_count // group, step, 0)


def write_letters(fills_ref, dest_ref, slot_ref, rows_ref, w_out_ref, proj, last, message):
    block_count, length = slot_ref.shape
    unique, width = rows_ref.shape
    fills = fills_ref[...]
    fill_col = column_of(fills.astype(F32)).astype(jnp.int32)
    last_slot = jnp.sum(
        jnp.where(iota((block_count, length), 1) == fill_col - 1, slot_ref[...].astype(F32), 0.0),
        axis=1,
        keepdims=True,
    ).astype(jnp.int32)
    pick = onehot(iota((block_count, unique), 1) == last_slot)
    gated = (last[...] * dot(pick, proj[:, :width])).astype(BF16)
    summary = (dot(pick, rows_ref[...]) + dot(gated, w_out_ref[...])).astype(BF16)
    row = iota((message.shape[0], block_count), 0)
    chosen = (row // PACK == dest_ref[...]) & (fills > 0)
    flag = jnp.sum(
        jnp.where(chosen & (row % PACK == width // LANES), 1.0, 0.0), axis=1, keepdims=True
    )
    letter = jnp.broadcast_to(flag, message.shape)
    for i in range(width // LANES):
        letter = letter + dot(
            onehot(chosen & (row % PACK == i)), summary[:, i * LANES : (i + 1) * LANES]
        )
    message[...] = letter.astype(BF16)


def read_letters(letters, summary_ref):
    rows = letters.shape[0]
    work, width = summary_ref.shape
    row, col = iota((rows, rows), 0), iota((rows, rows), 1)
    flag_col = col % PACK == width // LANES
    rank = dot(onehot(flag_col & (col // PACK < row // PACK)), letters[...])
    present = dot(onehot(flag_col & (col // PACK == row // PACK)), letters[...])
    wanted = (present > 0.5) & (rank.astype(jnp.int32) == iota((rows, LANES), 1))
    kind = iota((rows, LANES), 0) % PACK
    for i in range(width // LANES):
        part = dot(onehot(wanted & (kind == i)), letters[...], 0, 0)
        summary_ref[:, i * LANES : (i + 1) * LANES] = part[:work, :].astype(BF16)


def finish(w_in_ref, gain_in_ref, tall, spread, slope, hat, inv, dproj, grads):
    unique, width = hat.shape
    cols = slope.shape[1]
    parts, part_width = grads.shape[0], grads.shape[2]
    tile = min(FINISH_ROWS, unique)
    for r in range(0, unique, tile):
        rows = slice(r, r + tile)
        for c in range(0, cols, width):
            total = dot(tall[rows, :], spread[:, c : c + width])
            dproj[:, c : c + width] = (total * slope[rows, c : c + width]).astype(BF16)
        straight = dot(tall[rows, :], spread[:, cols:])
        dhat = dot(dproj[...], w_in_ref[...], 1, 1) * gain_in_ref[...]
        normal = hat[rows, :]
        scale = inv[rows, :1]
        mean = jnp.mean(dhat, axis=1, keepdims=True)
        along = jnp.mean(dhat * normal, axis=1, keepdims=True)
        dx = (scale * (dhat - mean - normal * along) + straight).astype(BF16)
        for p in range(parts):
            grads[p, rows, :] = dx[:, p * part_width : (p + 1) * part_width]


def step_kernel(
    dp_count,
    fill_ref, ids_ref, slot_ref, fills_ref, dest_ref, gain_in_ref, gain_out_ref,
    table_ref, aims_ref, w_in_hbm, w_out_hbm,
    summary_ref, total_ref,
    table_v, w_in_ref, w_out_ref, order, local, picks, picks_in, sorted_rows, served, rows_ref,
    here, tall, spread, dgated, proj, slope, hat, inv, normals, last, dproj,
    message, letters, grads, home, ordered, arrived,
    table_sem, load_sem, row_sems, pick_sems, letter_sems, home_sems, total_sems,
):
    table_count, cap = ids_ref.shape
    shard_rows, width = table_ref.shape
    cols = w_in_ref.shape[1]
    unique = table_count * cap
    run = shard_rows // dp_count
    length = slot_ref.shape[1]
    group = min(8, dp_count)
    span, part = group * run, group * 2 * table_count
    loads = [
        pltpu.make_async_copy(
            table_ref.at[pl.ds(g * span, span)], table_v.at[pl.ds(g * span, span)], table_sem.at[g]
        )
        for g in range(dp_count // group)
    ]
    w_out_load = pltpu.make_async_copy(w_out_hbm, w_out_ref, load_sem.at[0])
    aims_load = pltpu.make_async_copy(
        aims_ref, spread.at[:, pl.ds(cols, width)], load_sem.at[1]
    )
    w_in_load = pltpu.make_async_copy(w_in_hbm, w_in_ref, load_sem.at[2])
    for load in loads + [w_out_load, aims_load, w_in_load]:
        load.start()
    barrier = pltpu.get_barrier_semaphore()
    greet(barrier, dp_count, table_count)

    def pair(sems):
        return sems.at[0], sems.at[1]

    fill_order(ids_ref, order, local, run)
    index = dot(order[...], local[...], 0, 0)
    picks[...] = onehot(index.astype(jnp.int32) == iota((unique, run), 1))
    for g, load in enumerate(loads):
        mine = picks[g * part : (g + 1) * part, :]
        wide = jnp.concatenate([mine] * group, axis=1)
        same = iota((part, span), 0) // (2 * table_count) == iota((part, span), 1) // run
        load.wait()
        sorted_rows[g * part : (g + 1) * part, :] = dot(
            jnp.where(same, wide, jnp.zeros_like(wide)), table_v[g * span : (g + 1) * span, :]
        ).astype(BF16)
    served[...] = dot(order[...], sorted_rows[...]).astype(BF16)
    pl.semaphore_wait(barrier, dp_count + table_count - 2)
    row_exchange = Exchange("table", table_count, served, rows_ref, cap, pair(row_sems))
    row_exchange.start()
    pick_exchange = Exchange("dp", dp_count, picks, picks_in, 2 * table_count, pair(pick_sems))
    pick_exchange.start()

    w_out_load.wait()
    aims_load.wait()
    prepare(fill_ref, slot_ref, w_out_ref, here, tall, spread, dgated)
    w_in_load.wait()
    row_exchange.wait_recv()
    project(rows_ref, w_in_ref, gain_in_ref, gain_out_ref, length, proj, slope, hat, inv)
    gather(here, proj, spread)
    attend(fill_ref, length, spread, dgated, normals, last)
    write_letters(fills_ref, dest_ref, slot_ref, rows_ref, w_out_ref, proj, last, message)
    letter_exchange = Exchange("dp", dp_count, message, letters, PACK, pair(letter_sems))
    letter_exchange.start()
    finish(w_in_ref, gain_in_ref, tall, spread, slope, hat, inv, dproj, grads)

    parts = grads.shape[0]
    part_width = width // parts
    homes, totals = [], []
    for p in range(parts):
        homes.append(
            Exchange("table", table_count, grads.at[p], home.at[p], cap, pair(home_sems.at[p]))
        )
        totals.append(
            Exchange(
                "dp", dp_count, ordered.at[p], arrived.at[p], 2 * table_count, pair(total_sems.at[p])
            )
        )
        homes[p].start()
    for p in range(parts):
        homes[p].wait_recv()
        ordered[p, :, :] = dot(order[...], home[p, :, :], 0, 0).astype(BF16)
        totals[p].start()
    letter_exchange.wait_recv()
    read_letters(letters, summary_ref)
    pick_exchange.wait_recv()
    for p in range(parts):
        totals[p].wait_recv()
        total_ref[:, p * part_width : (p + 1) * part_width] = dot(
            picks_in[...], arrived[p, :, :], 0, 0
        )
    for exchange in [row_exchange, pick_exchange, letter_exchange] + homes + totals:
        exchange.wait_send()


def whole(space=pltpu.VMEM):
    return pl.BlockSpec(memory_space=space)


def body(
    embedding_table, served_ids, event_slot, block_fill, destination, target, w_in, w_out,
    gain_in, gain_out,
):
    dp_count, table_count = lax.axis_size("dp"), lax.axis_size("table")
    shard_rows, width = embedding_table.shape
    ids = served_ids[0, 0]
    cap = ids.shape[1]
    unique = table_count * cap
    run = shard_rows // dp_count
    slots = event_slot[0, 0]
    block_count, length = slots.shape
    work_count = block_count // 2
    events = block_count * length
    cols = w_in.shape[1]
    parts, part_width = PARTS, width // PARTS
    dma = pltpu.SemaphoreType.DMA
    vmem = pltpu.VMEM
    fills = block_fill[0, 0]
    summary, total = pl.pallas_call(
        functools.partial(step_kernel, dp_count),
        out_shape=(
            jax.ShapeDtypeStruct((work_count, width), BF16),
            jax.ShapeDtypeStruct((run, width), F32),
        ),
        in_specs=[whole(pltpu.SMEM)] + [whole()] * 6 + [whole(pl.ANY)] * 4,
        out_specs=(whole(), whole()),
        scratch_shapes=[
            vmem((shard_rows, width), BF16),
            vmem((width, cols), BF16),
            vmem((width, width), BF16),
            vmem((unique, unique), BF16),
            vmem((unique, run), BF16),
            vmem((unique, run), BF16),
            vmem((unique, run), BF16),
            vmem((unique, width), BF16),
            vmem((unique, width), BF16),
            vmem((unique, width), BF16),
        ]
        + compute_scratch(unique, events, cols, width, block_count, length)
        + [
            vmem((dp_count * PACK, LANES), BF16),
            vmem((dp_count * PACK, LANES), BF16),
            vmem((parts, unique, part_width), BF16),
            vmem((parts, unique, part_width), BF16),
            vmem((parts, unique, part_width), BF16),
            vmem((parts, unique, part_width), BF16),
            dma((max(1, dp_count // 8),)),
            dma((3,)),
            dma((2, table_count)),
            dma((2, dp_count)),
            dma((2, dp_count)),
            dma((parts, 2, table_count)),
            dma((parts, 2, dp_count)),
        ],
        compiler_params=pltpu.CompilerParams(
            vmem_limit_bytes=VMEM_BYTES, collective_id=0, has_side_effects=True
        ),
        name="step",
    )(
        fills, ids, slots, fills.reshape(1, -1), destination[0, 0].reshape(1, -1),
        gain_in.reshape(1, -1), gain_out.reshape(1, -1),
        embedding_table, target.reshape(events, width), w_in, w_out,
    )
    return (summary.reshape(1, 1, work_count, width), total.reshape(1, run, width))


def compute_scratch(unique, events, cols, width, block_count, length):
    vmem = pltpu.VMEM
    return [
        vmem((events, unique), BF16),
        vmem((unique, events), BF16),
        vmem((events, cols + width), BF16),
        vmem((events, width), BF16),
        vmem((unique, cols), BF16),
        vmem((unique, cols), F32),
        vmem((unique, width), F32),
        vmem((unique, LANES), F32),
        vmem((BLOCK_GROUP * length, width), F32),
        vmem((block_count, width), F32),
        vmem((min(FINISH_ROWS, unique), cols), BF16),
    ]


def solution(mesh):
    return jax.shard_map(
        body,
        mesh=mesh,
        in_specs=(
            P("table", None),
            P("dp", "table", None, None),
            P("dp", "table", None, None),
            P("dp", "table", None),
            P("dp", "table", None),
            P("dp", "table", None, None, None),
            P(), P(), P(), P(),
        ),
        out_specs=(P("dp", "table", None, None), P("table", "dp", None)),
        check_vma=False,
    )
```

time: 92.8 us -> 79.8 us (0.86)
  Pallas kernels: 87 us -> 69.4 us
  local copies, waits for them, and re-layouts: 4.89 us -> 9.39 us
    pallas_call x3 -> x1, Pallas kernels: 87 us -> 69.4 us  [body(): pl.pallas_call(functools.partial(step_kernel, dp_count), out_shape=(jax.S...]
    unnamed x22 -> x20, local copies, waits for them, and re-layouts: 4.89 us -> 9.39 us
where the time goes in v2:
time: 79.8 us; the launch traced here: 79.5 us
  Pallas kernels  69.4 us (87%)
  local copies, waits for them, and re-layouts  9.39 us (12%)
    pallas_call x1, Pallas kernels, body(): pl.pallas_call(functools.partial(step_kernel, dp_count), out_shape=(jax.S...  69.4 us
    unnamed x20, local copies, waits for them, and re-layouts  9.39 us

profile of v2, /device:TPU:1, one launch (start us, length us, event | category | flops | bytes accessed | tf_op | source)
XLA Modules:
  0.0 79.5 jit_solution(14493155001227027980)
XLA Ops:
  0.6 0.0 copy-start
  0.6 1.6 %copy-done = bf16[1,1,16,128,512]{4,3,2,1,0:T(8,128)(2,1)S(1)} copy-done((bf16[1,1,16,128,512]{4,3,2,1,0:T(8,128)(2,1)S(1)}, bf16[1,1,16,128,512]{4,3,2,1,0:T(8,128)(2,1)}, u32[]{:S(2)}) %copy-start) | copy-done | bytes 2097176
  2.2 0.0 copy-start.1
  2.2 1.4 %copy-done.1 = bf16[512,1536]{1,0:T(8,128)(2,1)S(1)} copy-done((bf16[512,1536]{1,0:T(8,128)(2,1)S(1)}, bf16[512,1536]{1,0:T(8,128)(2,1)}, u32[]{:S(2)}) %copy-start.1) | copy-done | bytes 1572888
  3.6 0.0 copy-start.2
  3.6 1.0 %copy-done.2 = bf16[512,512]{1,0:T(8,128)(2,1)S(1)} copy-done((bf16[512,512]{1,0:T(8,128)(2,1)S(1)}, bf16[512,512]{1,0:T(8,128)(2,1)}, u32[]{:S(2)}) %copy-start.2) | copy-done | bytes 524312
  4.7 0.0 copy-start.3
  4.7 0.7 copy-done.3
  5.4 0.0 copy-start.4
  5.4 0.7 copy-done.4
  6.1 0.0 copy-start.5
  6.1 0.7 copy-done.5
  6.7 0.0 copy-start.6
  6.7 0.7 copy-done.6
  7.4 0.0 copy-start.7
  7.4 0.7 copy-done.7
  8.1 0.0 copy-start.8
  8.1 0.7 copy-done.8
  8.7 69.4 %step.1 = (bf16[8,512]{1,0:T(8,128)(2,1)S(1)}, f32[128,512]{1,0:T(8,128)S(1)}) custom-call(s32[16]{0:T(128)S(1)} %bitcast.17, s32[8,64]{1,0:T(8,128)S(1)} %bitcast.14, s32[16,128]{1,0:T(8,128)S(1)} %bitcast.12, s32[1,16]{1,0:T(1,128)S(1)} %bitcast.18, s32[1,16]{1,0:T(1,128)S(1)} %bitcast.19, f32[1,512]{1,0:T(1,128)S(1)} %bitcast.15, f32[1,512]{1,0:T(1,128)S(1)} %bitcast.16, ...), custom_call_target="tpu_custom_call" | custom-call | tf_op jit(solution)/shard_map/step/pallas_call | solution.py:447
  78.2 0.6 copy.14
  78.8 0.7 copy.15
Async XLA Ops:
  0.6 1.6 %copy-start = (bf16[1,1,16,128,512]{4,3,2,1,0:T(8,128)(2,1)S(1)}, bf16[1,1,16,128,512]{4,3,2,1,0:T(8,128)(2,1)}, u32[]{:S(2)}) copy-start(bf16[1,1,16,128,512]{4,3,2,1,0:T(8,128)(2,1)} %param.15) | copy-start | bytes 6291460
  2.2 1.4 %copy-start.1 = (bf16[512,1536]{1,0:T(8,128)(2,1)S(1)}, bf16[512,1536]{1,0:T(8,128)(2,1)}, u32[]{:S(2)}) copy-start(bf16[512,1536]{1,0:T(8,128)(2,1)} %w_in_hbm.1) | copy-start | bytes 4718596
  3.6 1.0 %copy-start.2 = (bf16[512,512]{1,0:T(8,128)(2,1)S(1)}, bf16[512,512]{1,0:T(8,128)(2,1)}, u32[]{:S(2)}) copy-start(bf16[512,512]{1,0:T(8,128)(2,1)} %w_out_hbm.1) | copy-start | bytes 1572868
  4.7 0.7 copy-start.3
  5.4 0.7 copy-start.4
  6.1 0.7 copy-start.5
  6.7 0.7 copy-start.6
  7.4 0.7 copy-start.7
  8.1 0.7 copy-start.8

commit v3 on v2

--- a/solution.py
+++ b/solution.py
@@ -14,10 +14,10 @@
 EPS = 1e-05
 F32 = jnp.float32
 BF16 = jnp.bfloat16
-VMEM_BYTES = 48 * 1024 * 1024
-PROJECT_ROWS = 128
-GATHER_ROWS = 256
-BLOCK_GROUP = 2
+VMEM_BYTES = 60 * 1024 * 1024
+PROJECT_ROWS = 512
+GATHER_ROWS = 1024
+BLOCK_GROUP = 4
 FINISH_ROWS = 256
 PARTS = 2
 
@@ -109,12 +109,10 @@
         self.loop(lambda peer: self.copy(peer, self.me).wait_send())
 
 
-def prepare(fill_ref, slot_ref, w_out_ref, here, tall, spread, dgated):
+def prepare(slot_ref, here, tall):
     block_count, length = slot_ref.shape
     unique = here.shape[1]
-    cols = spread.shape[1] - w_out_ref.shape[0]
     eye = iota((length, length), 0) == iota((length, length), 1)
-    position = iota((length, 1), 0)
 
     def one(b, carry):
         rows = pl.ds(pl.multiple_of(b * length, length), length)
@@ -124,13 +122,25 @@
         ).astype(jnp.int32)
         here[rows, :] = onehot(iota((length, unique), 1) == slot_col)
         tall[:, rows] = onehot(iota((unique, length), 0) == slot_row)
+        return carry
+
+    lax.fori_loop(0, block_count, one, 0)
+
+
+def weigh(fill_ref, length, w_out_ref, spread, dgated):
+    events, width = dgated.shape
+    cols = spread.shape[1] - width
+    position = iota((length, 1), 0)
+
+    def one(b, carry):
+        rows = pl.ds(pl.multiple_of(b * length, length), length)
         aim = spread[rows, cols:]
         live_aim = jnp.where(position < fill_ref[b], aim, jnp.zeros_like(aim))
         spread[rows, cols:] = live_aim
         dgated[rows, :] = dot(live_aim, w_out_ref[...], 1, 1).astype(BF16)
         return carry
 
-    lax.fori_loop(0, block_count, one, 0)
+    lax.fori_loop(0, events // length, one, 0)
 
 
 def project(rows_ref, w_in_ref, gain_in_ref, gain_out_ref, length, proj, slope, hat, inv):
@@ -353,7 +363,7 @@
         aims_ref, spread.at[:, pl.ds(cols, width)], load_sem.at[1]
     )
     w_in_load = pltpu.make_async_copy(w_in_hbm, w_in_ref, load_sem.at[2])
-    for load in loads + [w_out_load, aims_load, w_in_load]:
+    for load in loads:
         load.start()
     barrier = pltpu.get_barrier_semaphore()
     greet(barrier, dp_count, table_count)
@@ -369,6 +379,9 @@
         wide = jnp.concatenate([mine] * group, axis=1)
         same = iota((part, span), 0) // (2 * table_count) == iota((part, span), 1) // run
         load.wait()
+        if g == max(0, len(loads) - 2):
+            for later in (w_out_load, aims_load, w_in_load):
+                later.start()
         sorted_rows[g * part : (g + 1) * part, :] = dot(
             jnp.where(same, wide, jnp.zeros_like(wide)), table_v[g * span : (g + 1) * span, :]
         ).astype(BF16)
@@ -379,9 +392,10 @@
     pick_exchange = Exchange("dp", dp_count, picks, picks_in, 2 * table_count, pair(pick_sems))
     pick_exchange.start()
 
+    prepare(slot_ref, here, tall)
     w_out_load.wait()
     aims_load.wait()
-    prepare(fill_ref, slot_ref, w_out_ref, here, tall, spread, dgated)
+    weigh(fill_ref, length, w_out_ref, spread, dgated)
     w_in_load.wait()
     row_exchange.wait_recv()
     project(rows_ref, w_in_ref, gain_in_ref, gain_out_ref, length, proj, slope, hat, inv)

time: 79.8 us -> 72.5 us (0.909)
  local copies, waits for them, and re-layouts: 9.39 us -> 2.97 us
    unnamed x20 -> x2, local copies, waits for them, and re-layouts: 9.39 us -> 2.97 us
where the time goes in v3:
time: 72.5 us; the launch traced here: 72.4 us
  Pallas kernels  68.7 us (95%)
  local copies, waits for them, and re-layouts  2.97 us (4%)
    pallas_call x1, Pallas kernels, body(): pl.pallas_call(functools.partial(step_kernel, dp_count), out_shape=(jax.S...  68.7 us
    unnamed x2, local copies, waits for them, and re-layouts  2.97 us

profile of v3, /device:TPU:1, one launch (start us, length us, event | category | flops | bytes accessed | tf_op | source)
XLA Modules:
  0.0 72.4 jit_solution(4646906507961520576)
XLA Ops:
  0.6 68.7 %step.1 = (bf16[8,512]{1,0:T(8,128)(2,1)}, f32[128,512]{1,0:T(8,128)}) custom-call(s32[16]{0:T(128)} %bitcast.17, s32[8,64]{1,0:T(8,128)} %bitcast.14, s32[16,128]{1,0:T(8,128)} %bitcast.12, s32[1,16]{1,0:T(1,128)} %bitcast.18, s32[1,16]{1,0:T(1,128)} %bitcast.19, f32[1,512]{1,0:T(1,128)} %bitcast.15, f32[1,512]{1,0:T(1,128)} %bitcast.16, ...), custom_call_target="tpu_custom_call" | custom-call | tf_op jit(solution)/shard_map/step/pallas_call | solution.py:461
  69.4 1.3 %copy.14 = bf16[1,1,8,512]{3,2,1,0:T(8,128)(2,1)} copy(bf16[1,1,8,512]{3,2,1,0:T(8,128)(2,1)} %bitcast.13) | data formatting | bytes 16384
  70.7 1.7 %copy.15 = f32[1,128,512]{2,1,0:T(8,128)} copy(f32[1,128,512]{2,1,0:T(8,128)} %bitcast.11) | data formatting | bytes 524288

commit v4 on v3

--- a/solution.py
+++ b/solution.py
@@ -15,10 +15,9 @@
 F32 = jnp.float32
 BF16 = jnp.bfloat16
 VMEM_BYTES = 60 * 1024 * 1024
-PROJECT_ROWS = 512
+PROJECT_ROWS = 256
 GATHER_ROWS = 1024
 BLOCK_GROUP = 4
-FINISH_ROWS = 256
 PARTS = 2
 
 
@@ -42,6 +41,11 @@
     n = row.shape[1]
     here = iota((n, n), 0) == iota((n, n), 1)
     return jnp.sum(jnp.where(here, row, 0.0), axis=1, keepdims=True)
+
+
+def halved(slot, cap, unique):
+    part = cap // 2
+    return (slot % cap) // part * (unique // 2) + slot // cap * part + slot % part
 
 
 def fill_order(ids_ref, order_ref, local_ref, run):
@@ -52,12 +56,15 @@
         column = column_of(row)
         rank = jnp.sum(jnp.where(row < column, 1.0, 0.0), axis=1, keepdims=True).astype(jnp.int32)
         place = (rank // 2) * (2 * table_count) + 2 * t + rank % 2
-        order_ref[t * cap : (t + 1) * cap, :] = onehot(iota((cap, unique), 1) == place)
-        if local_ref is not None:
-            local = column.astype(jnp.int32) % run
-            local_ref[t * cap : (t + 1) * cap, :] = jnp.broadcast_to(
-                local.astype(F32), (cap, run)
-            ).astype(BF16)
+        hot = onehot(iota((cap, unique), 1) == place)
+        local = (column.astype(jnp.int32) % run).astype(F32)
+        local = jnp.broadcast_to(local, (cap, run)).astype(BF16)
+        part = cap // 2
+        for half in range(2):
+            there = half * (unique // 2) + t * part
+            here = slice(half * part, (half + 1) * part)
+            order_ref[there : there + part, :] = hot[here, :]
+            local_ref[there : there + part, :] = local[here, :]
 
 
 def greet(barrier, dp_count, table_count):
@@ -143,17 +150,18 @@
     lax.fori_loop(0, events // length, one, 0)
 
 
-def project(rows_ref, w_in_ref, gain_in_ref, gain_out_ref, length, proj, slope, hat, inv):
+def project(half, rows_ref, w_in_ref, gain_in_ref, gain_out_ref, length, proj, slope, hat, inv):
     unique, width = rows_ref.shape
+    unique //= 2
     query = H * QK
     gain_in = gain_in_ref[...]
-    half = 0.5 * QK ** (-0.5)
+    tilt = 0.5 * QK ** (-0.5)
     lane = iota((1, 2 * query), 1)
-    factors = [gain_out_ref[...], 1.0 / length, jnp.where(lane < query, half, 1.0)]
+    factors = [gain_out_ref[...], 1.0 / length, jnp.where(lane < query, tilt, 1.0)]
     chunk = min(PROJECT_ROWS, unique)
 
     def step(i, carry):
-        rows = pl.ds(pl.multiple_of(i * chunk, chunk), chunk)
+        rows = pl.ds(pl.multiple_of(half * unique + i * chunk, chunk), chunk)
         x = rows_ref[rows, :].astype(F32)
         shifted = x - jnp.mean(x, axis=1, keepdims=True)
         scale = lax.rsqrt(jnp.mean(shifted * shifted, axis=1, keepdims=True) + EPS)
@@ -273,29 +281,33 @@
     lax.fori_loop(0, block_count // group, step, 0)
 
 
-def write_letters(fills_ref, dest_ref, slot_ref, rows_ref, w_out_ref, proj, last, message):
-    block_count, length = slot_ref.shape
-    unique, width = rows_ref.shape
+def address_letters(fills_ref, dest_ref, marks, pick, chosen, flag):
+    block_count, length = marks.shape
+    unique = pick.shape[1]
+    kinds = chosen.shape[0]
     fills = fills_ref[...]
     fill_col = column_of(fills.astype(F32)).astype(jnp.int32)
-    last_slot = jnp.sum(
-        jnp.where(iota((block_count, length), 1) == fill_col - 1, slot_ref[...].astype(F32), 0.0),
+    last_mark = jnp.sum(
+        jnp.where(iota((block_count, length), 1) == fill_col - 1, marks[...].astype(F32), 0.0),
         axis=1,
         keepdims=True,
     ).astype(jnp.int32)
-    pick = onehot(iota((block_count, unique), 1) == last_slot)
-    gated = (last[...] * dot(pick, proj[:, :width])).astype(BF16)
-    summary = (dot(pick, rows_ref[...]) + dot(gated, w_out_ref[...])).astype(BF16)
-    row = iota((message.shape[0], block_count), 0)
-    chosen = (row // PACK == dest_ref[...]) & (fills > 0)
-    flag = jnp.sum(
-        jnp.where(chosen & (row % PACK == width // LANES), 1.0, 0.0), axis=1, keepdims=True
-    )
-    letter = jnp.broadcast_to(flag, message.shape)
-    for i in range(width // LANES):
-        letter = letter + dot(
-            onehot(chosen & (row % PACK == i)), summary[:, i * LANES : (i + 1) * LANES]
-        )
+    pick[...] = onehot(iota((block_count, unique), 1) == last_mark)
+    row = iota((flag.shape[0], block_count), 0)
+    mine = (row // PACK == dest_ref[...]) & (fills > 0)
+    present = jnp.sum(jnp.where(mine & (row % PACK == kinds), 1.0, 0.0), axis=1, keepdims=True)
+    flag[...] = jnp.broadcast_to(present, flag.shape).astype(BF16)
+    for i in range(kinds):
+        chosen[i, :, :] = onehot(mine & (row % PACK == i))
+
+
+def write_letters(rows_ref, w_out_ref, proj, last, pick, chosen, flag, message):
+    width = rows_ref.shape[1]
+    gated = (last[...] * dot(pick[...], proj[:, :width])).astype(BF16)
+    summary = (dot(pick[...], rows_ref[...]) + dot(gated, w_out_ref[...])).astype(BF16)
+    letter = flag[...].astype(F32)
+    for i in range(chosen.shape[0]):
+        letter = letter + dot(chosen[i, :, :], summary[:, i * LANES : (i + 1) * LANES])
     message[...] = letter.astype(BF16)
 
 
@@ -313,25 +325,24 @@
         summary_ref[:, i * LANES : (i + 1) * LANES] = part[:work, :].astype(BF16)
 
 
-def finish(w_in_ref, gain_in_ref, tall, spread, slope, hat, inv, dproj, grads):
+def finish(half, w_in_ref, gain_in_ref, tall, spread, slope, hat, inv, dproj, grads):
     unique, width = hat.shape
     cols = slope.shape[1]
     parts, part_width = grads.shape[0], grads.shape[2]
-    tile = min(FINISH_ROWS, unique)
-    for r in range(0, unique, tile):
-        rows = slice(r, r + tile)
-        for c in range(0, cols, width):
-            total = dot(tall[rows, :], spread[:, c : c + width])
-            dproj[:, c : c + width] = (total * slope[rows, c : c + width]).astype(BF16)
-        straight = dot(tall[rows, :], spread[:, cols:])
-        dhat = dot(dproj[...], w_in_ref[...], 1, 1) * gain_in_ref[...]
-        normal = hat[rows, :]
-        scale = inv[rows, :1]
-        mean = jnp.mean(dhat, axis=1, keepdims=True)
-        along = jnp.mean(dhat * normal, axis=1, keepdims=True)
-        dx = (scale * (dhat - mean - normal * along) + straight).astype(BF16)
-        for p in range(parts):
-            grads[p, rows, :] = dx[:, p * part_width : (p + 1) * part_width]
+    tile = unique // 2
+    rows = slice(half * tile, (half + 1) * tile)
+    for c in range(0, cols, width):
+        total = dot(tall[rows, :], spread[:, c : c + width])
+        dproj[:, c : c + width] = (total * slope[rows, c : c + width]).astype(BF16)
+    straight = dot(tall[rows, :], spread[:, cols:])
+    dhat = dot(dproj[...], w_in_ref[...], 1, 1) * gain_in_ref[...]
+    normal = hat[rows, :]
+    scale = inv[rows, :1]
+    mean = jnp.mean(dhat, axis=1, keepdims=True)
+    along = jnp.mean(dhat * normal, axis=1, keepdims=True)
+    dx = (scale * (dhat - mean - normal * along) + straight).astype(BF16)
+    for p in range(parts):
+        grads[p, rows, :] = dx[:, p * part_width : (p + 1) * part_width]
 
 
 def step_kernel(
@@ -341,7 +352,7 @@
     summary_ref, total_ref,
     table_v, w_in_ref, w_out_ref, order, local, picks, picks_in, sorted_rows, served, rows_ref,
     here, tall, spread, dgated, proj, slope, hat, inv, normals, last, dproj,
-    message, letters, grads, home, ordered, arrived,
+    marks, pick, chosen, flag, message, letters, grads, home, ordered, arrived,
     table_sem, load_sem, row_sems, pick_sems, letter_sems, home_sems, total_sems,
 ):
     table_count, cap = ids_ref.shape
@@ -387,41 +398,58 @@
         ).astype(BF16)
     served[...] = dot(order[...], sorted_rows[...]).astype(BF16)
     pl.semaphore_wait(barrier, dp_count + table_count - 2)
-    row_exchange = Exchange("table", table_count, served, rows_ref, cap, pair(row_sems))
-    row_exchange.start()
+    halves = [pl.ds(half * (unique // 2), unique // 2) for half in range(2)]
+    row_exchanges = [
+        Exchange(
+            "table", table_count, served.at[rows], rows_ref.at[rows], cap // 2, pair(row_sems.at[half])
+        )
+        for half, rows in enumerate(halves)
+    ]
+    for exchange in row_exchanges:
+        exchange.start()
     pick_exchange = Exchange("dp", dp_count, picks, picks_in, 2 * table_count, pair(pick_sems))
     pick_exchange.start()
 
-    prepare(slot_ref, here, tall)
+    marks[...] = halved(slot_ref[...], cap, unique)
+    prepare(marks, here, tall)
+    address_letters(fills_ref, dest_ref, marks, pick, chosen, flag)
     w_out_load.wait()
     aims_load.wait()
     weigh(fill_ref, length, w_out_ref, spread, dgated)
     w_in_load.wait()
-    row_exchange.wait_recv()
-    project(rows_ref, w_in_ref, gain_in_ref, gain_out_ref, length, proj, slope, hat, inv)
+    for half, exchange in enumerate(row_exchanges):
+        exchange.wait_recv()
+        project(
+            half, rows_ref, w_in_ref, gain_in_ref, gain_out_ref, length, proj, slope, hat, inv
+        )
     gather(here, proj, spread)
     attend(fill_ref, length, spread, dgated, normals, last)
-    write_letters(fills_ref, dest_ref, slot_ref, rows_ref, w_out_ref, proj, last, message)
-    letter_exchange = Exchange("dp", dp_count, message, letters, PACK, pair(letter_sems))
-    letter_exchange.start()
-    finish(w_in_ref, gain_in_ref, tall, spread, slope, hat, inv, dproj, grads)
+    write_letters(rows_ref, w_out_ref, proj, last, pick, chosen, flag, message)
 
     parts = grads.shape[0]
     part_width = width // parts
+    letter_exchange = Exchange("dp", dp_count, message, letters, PACK, pair(letter_sems))
     homes, totals = [], []
+    for half, rows in enumerate(halves):
+        finish(half, w_in_ref, gain_in_ref, tall, spread, slope, hat, inv, dproj, grads)
+        for p in range(parts):
+            home_exchange = Exchange(
+                "table", table_count, grads.at[p, rows], home.at[p, rows], cap // 2,
+                pair(home_sems.at[half, p]),
+            )
+            home_exchange.start()
+            homes.append(home_exchange)
+        if half == 0:
+            letter_exchange.start()
     for p in range(parts):
-        homes.append(
-            Exchange("table", table_count, grads.at[p], home.at[p], cap, pair(home_sems.at[p]))
-        )
+        homes[p].wait_recv()
+        homes[parts + p].wait_recv()
+        ordered[p, :, :] = dot(order[...], home[p, :, :], 0, 0).astype(BF16)
         totals.append(
             Exchange(
                 "dp", dp_count, ordered.at[p], arrived.at[p], 2 * table_count, pair(total_sems.at[p])
             )
         )
-        homes[p].start()
-    for p in range(parts):
-        homes[p].wait_recv()
-        ordered[p, :, :] = dot(order[...], home[p, :, :], 0, 0).astype(BF16)
         totals[p].start()
     letter_exchange.wait_recv()
     read_letters(letters, summary_ref)
@@ -431,8 +459,19 @@
         total_ref[:, p * part_width : (p + 1) * part_width] = dot(
             picks_in[...], arrived[p, :, :], 0, 0
         )
-    for exchange in [row_exchange, pick_exchange, letter_exchange] + homes + totals:
+    for exchange in row_exchanges + [pick_exchange, letter_exchange] + homes + totals:
         exchange.wait_send()
+
+
+def hand_on(summary_in, total_in, summary_out, total_out, sems):
+    copies = [
+        pltpu.make_async_copy(summary_in, summary_out, sems.at[0]),
+        pltpu.make_async_copy(total_in, total_out, sems.at[1]),
+    ]
+    for copy in copies:
+        copy.start()
+    for copy in copies:
+        copy.wait()
 
 
 def whole(space=pltpu.VMEM):
@@ -480,6 +519,10 @@
         ]
         + compute_scratch(unique, events, cols, width, block_count, length)
         + [
+            vmem((block_count, length), jnp.int32),
+            vmem((block_count, unique), BF16),
+            vmem((width // LANES, dp_count * PACK, block_count), BF16),
+            vmem((dp_count * PACK, LANES), BF16),
             vmem((dp_count * PACK, LANES), BF16),
             vmem((dp_count * PACK, LANES), BF16),
             vmem((parts, unique, part_width), BF16),
@@ -488,10 +531,10 @@
             vmem((parts, unique, part_width), BF16),
             dma((max(1, dp_count // 8),)),
             dma((3,)),
-            dma((2, table_count)),
+            dma((2, 2, table_count)),
             dma((2, dp_count)),
             dma((2, dp_count)),
-            dma((parts, 2, table_count)),
+            dma((2, parts, 2, table_count)),
             dma((parts, 2, dp_count)),
         ],
         compiler_params=pltpu.CompilerParams(
@@ -503,6 +546,18 @@
         gain_in.reshape(1, -1), gain_out.reshape(1, -1),
         embedding_table, target.reshape(events, width), w_in, w_out,
     )
+    summary, total = pl.pallas_call(
+        hand_on,
+        out_shape=(
+            jax.ShapeDtypeStruct((work_count, width), BF16),
+            jax.ShapeDtypeStruct((run, width), F32),
+        ),
+        in_specs=[whole(pl.ANY)] * 2,
+        out_specs=(whole(pl.ANY), whole(pl.ANY)),
+        scratch_shapes=[dma((2,))],
+        compiler_params=pltpu.CompilerParams(vmem_limit_bytes=VMEM_BYTES),
+        name="hand_on",
+    )(summary, total)
     return (summary.reshape(1, 1, work_count, width), total.reshape(1, run, width))
 
 
@@ -519,7 +574,7 @@
         vmem((unique, LANES), F32),
         vmem((BLOCK_GROUP * length, width), F32),
         vmem((block_count, width), F32),
-        vmem((min(FINISH_ROWS, unique), cols), BF16),
+        vmem((unique // 2, cols), BF16),
     ]
 
 

time: 72.5 us -> 78.8 us (1.087)
  Pallas kernels: 68.7 us -> 77.9 us
  local copies, waits for them, and re-layouts: 2.97 us -> 0 us
    pallas_call x0 -> x1, Pallas kernels: none -> 9.31 us  [body(): pl.pallas_call(hand_on, out_shape=(jax.ShapeDtypeStruct((work_count, widt...]
    unnamed x2 -> x0, local copies, waits for them, and re-layouts: 2.97 us -> none
where the time goes in v4:
time: 78.8 us; the launch traced here: 78.7 us
  Pallas kernels  77.9 us (99%)
  between operations  0.8 us (1%)
    pallas_call x1, Pallas kernels, body(): pl.pallas_call(functools.partial(step_kernel, dp_count), out_shape=(jax.S...  68.5 us
    pallas_call x1, Pallas kernels, body(): pl.pallas_call(hand_on, out_shape=(jax.ShapeDtypeStruct((work_count, widt...  9.31 us

profile of v4, /device:TPU:1, one launch (start us, length us, event | category | flops | bytes accessed | tf_op | source)
XLA Modules:
  0.0 78.7 jit_solution(12202779828222030895)
XLA Ops:
  0.6 68.5 %step.1 = (bf16[8,512]{1,0:T(8,128)(2,1)}, f32[128,512]{1,0:T(8,128)}) custom-call(s32[16]{0:T(128)} %bitcast.15, s32[8,64]{1,0:T(8,128)} %bitcast.12, s32[16,128]{1,0:T(8,128)} %bitcast.11, s32[1,16]{1,0:T(1,128)} %bitcast.16, s32[1,16]{1,0:T(1,128)} %bitcast.17, f32[1,512]{1,0:T(1,128)} %bitcast.13, f32[1,512]{1,0:T(1,128)} %bitcast.14, ...), custom_call_target="tpu_custom_call" | custom-call | tf_op jit(solution)/shard_map/step/pallas_call | solution.py:500
  69.2 9.3 %hand_on.1 = (bf16[8,512]{1,0:T(8,128)(2,1)}, f32[128,512]{1,0:T(8,128)}) custom-call(bf16[8,512]{1,0:T(8,128)(2,1)} %get-tuple-element.6.summary_in, f32[128,512]{1,0:T(8,128)} %get-tuple-element.7.total_in), custom_call_target="tpu_custom_call" | custom-call | tf_op jit(solution)/shard_map/hand_on/pallas_call | solution.py:549

commit v5 on v4

--- a/solution.py
+++ b/solution.py
@@ -18,7 +18,7 @@
 PROJECT_ROWS = 256
 GATHER_ROWS = 1024
 BLOCK_GROUP = 4
-PARTS = 2
+PARTS = 1
 
 
 def dot(a, b, ca=1, cb=0):
@@ -93,8 +93,8 @@
         return pltpu.make_async_remote_copy(
             src_ref=self.source.at[self.rows(peer)],
             dst_ref=self.target.at[self.rows(slot)],
-            send_sem=self.send.at[peer],
-            recv_sem=self.recv.at[slot],
+            send_sem=self.send,
+            recv_sem=self.recv,
             device_id={self.axis: peer},
         )
 
@@ -109,11 +109,15 @@
         self.loop(lambda peer: self.copy(peer, self.me).start())
         self.target[self.rows(self.me), :] = self.source[self.rows(self.me), :]
 
+    def wait(self, sem):
+        rows = pl.ds(0, (self.count - 1) * self.block)
+        pltpu.make_async_copy(self.source.at[rows], self.target.at[rows], sem).wait()
+
     def wait_recv(self):
-        self.loop(lambda peer: self.copy(peer, peer).wait_recv())
+        self.wait(self.recv)
 
     def wait_send(self):
-        self.loop(lambda peer: self.copy(peer, self.me).wait_send())
+        self.wait(self.send)
 
 
 def prepare(slot_ref, here, tall):
@@ -454,24 +458,20 @@
     letter_exchange.wait_recv()
     read_letters(letters, summary_ref)
     pick_exchange.wait_recv()
+    for exchange in row_exchanges + [pick_exchange, letter_exchange] + homes:
+        exchange.wait_send()
     for p in range(parts):
         totals[p].wait_recv()
         total_ref[:, p * part_width : (p + 1) * part_width] = dot(
             picks_in[...], arrived[p, :, :], 0, 0
         )
-    for exchange in row_exchanges + [pick_exchange, letter_exchange] + homes + totals:
+    for exchange in totals:
         exchange.wait_send()
 
 
-def hand_on(summary_in, total_in, summary_out, total_out, sems):
-    copies = [
-        pltpu.make_async_copy(summary_in, summary_out, sems.at[0]),
-        pltpu.make_async_copy(total_in, total_out, sems.at[1]),
-    ]
-    for copy in copies:
-        copy.start()
-    for copy in copies:
-        copy.wait()
+def hand_on(summary_in, total_in, summary_out, total_out):
+    summary_out[...] = summary_in[...]
+    total_out[...] = total_in[...]
 
 
 def whole(space=pltpu.VMEM):
@@ -531,11 +531,11 @@
             vmem((parts, unique, part_width), BF16),
             dma((max(1, dp_count // 8),)),
             dma((3,)),
-            dma((2, 2, table_count)),
-            dma((2, dp_count)),
-            dma((2, dp_count)),
-            dma((2, parts, 2, table_count)),
-            dma((parts, 2, dp_count)),
+            dma((2, 2)),
+            dma((2,)),
+            dma((2,)),
+            dma((2, parts, 2)),
+            dma((parts, 2)),
         ],
         compiler_params=pltpu.CompilerParams(
             vmem_limit_bytes=VMEM_BYTES, collective_id=0, has_side_effects=True
@@ -552,9 +552,8 @@
             jax.ShapeDtypeStruct((work_count, width), BF16),
             jax.ShapeDtypeStruct((run, width), F32),
         ),
-        in_specs=[whole(pl.ANY)] * 2,
-        out_specs=(whole(pl.ANY), whole(pl.ANY)),
-        scratch_shapes=[dma((2,))],
+        in_specs=[whole()] * 2,
+        out_specs=(whole(), whole()),
         compiler_params=pltpu.CompilerParams(vmem_limit_bytes=VMEM_BYTES),
         name="hand_on",
     )(summary, total)

time: 78.8 us -> 65.7 us (0.83)
  Pallas kernels: 77.9 us -> 64.9 us
    pallas_call x1, Pallas kernels: 9.31 us -> 1.69 us  [body(): pl.pallas_call(hand_on, out_shape=(jax.ShapeDtypeStruct((work_count, widt...]
    pallas_call x1, Pallas kernels: 68.5 us -> 63.2 us  [body(): pl.pallas_call(functools.partial(step_kernel, dp_count), out_shape=(jax.S...]
where the time goes in v5:
time: 65.7 us; the launch traced here: 65.5 us
  Pallas kernels  64.9 us (99%)
    pallas_call x1, Pallas kernels, body(): pl.pallas_call(functools.partial(step_kernel, dp_count), out_shape=(jax.S...  63.2 us
    pallas_call x1, Pallas kernels, body(): pl.pallas_call(hand_on, out_shape=(jax.ShapeDtypeStruct((work_count, widt...  1.69 us

profile of v5, /device:TPU:1, one launch (start us, length us, event | category | flops | bytes accessed | tf_op | source)
XLA Modules:
  0.0 65.5 jit_solution(15310769106920664558)
XLA Ops:
  0.6 63.2 %step.1 = (bf16[8,512]{1,0:T(8,128)(2,1)}, f32[128,512]{1,0:T(8,128)}) custom-call(s32[16]{0:T(128)} %bitcast.15, s32[8,64]{1,0:T(8,128)} %bitcast.12, s32[16,128]{1,0:T(8,128)} %bitcast.11, s32[1,16]{1,0:T(1,128)} %bitcast.16, s32[1,16]{1,0:T(1,128)} %bitcast.17, f32[1,512]{1,0:T(1,128)} %bitcast.13, f32[1,512]{1,0:T(1,128)} %bitcast.14, ...), custom_call_target="tpu_custom_call" | custom-call | tf_op jit(solution)/shard_map/step/pallas_call | solution.py:500
  63.8 1.7 %hand_on.1 = (bf16[8,512]{1,0:T(8,128)(2,1)}, f32[128,512]{1,0:T(8,128)}) custom-call(bf16[8,512]{1,0:T(8,128)(2,1)} %get-tuple-element.6.summary_in, f32[128,512]{1,0:T(8,128)} %get-tuple-element.7.total_in), custom_call_target="tpu_custom_call" | custom-call | tf_op jit(solution)/shard_map/hand_on/pallas_call | solution.py:549

commit v6 on v5

--- a/solution.py
+++ b/solution.py
@@ -18,7 +18,6 @@
 PROJECT_ROWS = 256
 GATHER_ROWS = 1024
 BLOCK_GROUP = 4
-PARTS = 1
 
 
 def dot(a, b, ca=1, cb=0):
@@ -43,12 +42,20 @@
     return jnp.sum(jnp.where(here, row, 0.0), axis=1, keepdims=True)
 
 
-def halved(slot, cap, unique):
-    part = cap // 2
-    return (slot % cap) // part * (unique // 2) + slot // cap * part + slot % part
-
-
-def fill_order(ids_ref, order_ref, local_ref, run):
+def to_halves(unique, table_count):
+    part = unique // 2 // table_count
+    row, col = iota((unique, unique), 0), iota((unique, unique), 1)
+    half, t, place = row // (unique // 2), row // part % table_count, row % part
+    return onehot(col == (place // 2 * 2 + half) * (2 * table_count) + 2 * t + place % 2)
+
+
+def from_half(size, table_count):
+    row, col = iota((size, size), 0), iota((size, size), 1)
+    pack = 2 * table_count
+    return onehot(col == row % pack // 2 * (size // table_count) + row // pack * 2 + row % 2)
+
+
+def fill_order(ids_ref, order_ref, local_ref, label_ref, run):
     table_count, cap = ids_ref.shape
     unique = table_count * cap
     for t in range(table_count):
@@ -56,15 +63,11 @@
         column = column_of(row)
         rank = jnp.sum(jnp.where(row < column, 1.0, 0.0), axis=1, keepdims=True).astype(jnp.int32)
         place = (rank // 2) * (2 * table_count) + 2 * t + rank % 2
-        hot = onehot(iota((cap, unique), 1) == place)
+        rows = slice(t * cap, (t + 1) * cap)
+        order_ref[rows, :] = onehot(iota((cap, unique), 1) == place)
         local = (column.astype(jnp.int32) % run).astype(F32)
-        local = jnp.broadcast_to(local, (cap, run)).astype(BF16)
-        part = cap // 2
-        for half in range(2):
-            there = half * (unique // 2) + t * part
-            here = slice(half * part, (half + 1) * part)
-            order_ref[there : there + part, :] = hot[here, :]
-            local_ref[there : there + part, :] = local[here, :]
+        local_ref[rows, :] = jnp.broadcast_to(local, (cap, run)).astype(BF16)
+        label_ref[rows, :] = iota((cap, LANES), 0).astype(F32).astype(BF16)
 
 
 def greet(barrier, dp_count, table_count):
@@ -120,9 +123,14 @@
         self.wait(self.send)
 
 
-def prepare(slot_ref, here, tall):
+def prepare(slot_ref, labels_in, cap, here, tall, names, name_row):
     block_count, length = slot_ref.shape
     unique = here.shape[1]
+    part = cap // 2
+    owner = iota((unique, LANES), 0) % (unique // 2) // part
+    name = labels_in[...].astype(F32) + (owner * cap).astype(F32)
+    names[...] = name.astype(jnp.int32)
+    name_row[...] = jnp.transpose(name)[:8, :].astype(jnp.int32)
     eye = iota((length, length), 0) == iota((length, length), 1)
 
     def one(b, carry):
@@ -131,8 +139,8 @@
         slot_col = jnp.sum(
             jnp.where(eye, slot_row.astype(F32), 0.0), axis=1, keepdims=True
         ).astype(jnp.int32)
-        here[rows, :] = onehot(iota((length, unique), 1) == slot_col)
-        tall[:, rows] = onehot(iota((unique, length), 0) == slot_row)
+        here[rows, :] = onehot(name_row[:1, :] == slot_col)
+        tall[:, rows] = onehot(names[...] == slot_row)
         return carry
 
     lax.fori_loop(0, block_count, one, 0)
@@ -285,18 +293,17 @@
     lax.fori_loop(0, block_count // group, step, 0)
 
 
-def address_letters(fills_ref, dest_ref, marks, pick, chosen, flag):
-    block_count, length = marks.shape
-    unique = pick.shape[1]
+def address_letters(fills_ref, dest_ref, slot_ref, name_row, pick, chosen, flag):
+    block_count, length = slot_ref.shape
     kinds = chosen.shape[0]
     fills = fills_ref[...]
     fill_col = column_of(fills.astype(F32)).astype(jnp.int32)
-    last_mark = jnp.sum(
-        jnp.where(iota((block_count, length), 1) == fill_col - 1, marks[...].astype(F32), 0.0),
+    last_slot = jnp.sum(
+        jnp.where(iota((block_count, length), 1) == fill_col - 1, slot_ref[...].astype(F32), 0.0),
         axis=1,
         keepdims=True,
     ).astype(jnp.int32)
-    pick[...] = onehot(iota((block_count, unique), 1) == last_mark)
+    pick[...] = onehot(name_row[:1, :] == last_slot)
     row = iota((flag.shape[0], block_count), 0)
     mine = (row // PACK == dest_ref[...]) & (fills > 0)
     present = jnp.sum(jnp.where(mine & (row % PACK == kinds), 1.0, 0.0), axis=1, keepdims=True)
@@ -332,7 +339,6 @@
 def finish(half, w_in_ref, gain_in_ref, tall, spread, slope, hat, inv, dproj, grads):
     unique, width = hat.shape
     cols = slope.shape[1]
-    parts, part_width = grads.shape[0], grads.shape[2]
     tile = unique // 2
     rows = slice(half * tile, (half + 1) * tile)
     for c in range(0, cols, width):
@@ -345,8 +351,7 @@
     mean = jnp.mean(dhat, axis=1, keepdims=True)
     along = jnp.mean(dhat * normal, axis=1, keepdims=True)
     dx = (scale * (dhat - mean - normal * along) + straight).astype(BF16)
-    for p in range(parts):
-        grads[p, rows, :] = dx[:, p * part_width : (p + 1) * part_width]
+    grads[rows, :] = dx
 
 
 def step_kernel(
@@ -356,8 +361,8 @@
     summary_ref, total_ref,
     table_v, w_in_ref, w_out_ref, order, local, picks, picks_in, sorted_rows, served, rows_ref,
     here, tall, spread, dgated, proj, slope, hat, inv, normals, last, dproj,
-    marks, pick, chosen, flag, message, letters, grads, home, ordered, arrived,
-    table_sem, load_sem, row_sems, pick_sems, letter_sems, home_sems, total_sems,
+    labels, labels_out, labels_in, shift, names, name_row, pick, chosen, flag, message, letters, grads, home, ordered, arrived,
+    table_sem, load_sem, label_sems, row_sems, pick_sems, letter_sems, home_sems, total_sems,
 ):
     table_count, cap = ids_ref.shape
     shard_rows, width = table_ref.shape
@@ -386,9 +391,23 @@
     def pair(sems):
         return sems.at[0], sems.at[1]
 
-    fill_order(ids_ref, order, local, run)
+    fill_order(ids_ref, order, local, labels, run)
     index = dot(order[...], local[...], 0, 0)
     picks[...] = onehot(index.astype(jnp.int32) == iota((unique, run), 1))
+    shift[...] = to_halves(unique, table_count)
+    placed = dot(order[...], labels[...], 0, 0).astype(BF16)
+    labels_out[...] = dot(shift[...], placed).astype(BF16)
+    pl.semaphore_wait(barrier, dp_count + table_count - 2)
+    halves = [pl.ds(half * (unique // 2), unique // 2) for half in range(2)]
+    label_exchanges = [
+        Exchange(
+            "table", table_count, labels_out.at[rows], labels_in.at[rows], cap // 2,
+            pair(label_sems.at[half]),
+        )
+        for half, rows in enumerate(halves)
+    ]
+    for exchange in label_exchanges:
+        exchange.start()
     for g, load in enumerate(loads):
         mine = picks[g * part : (g + 1) * part, :]
         wide = jnp.concatenate([mine] * group, axis=1)
@@ -400,9 +419,7 @@
         sorted_rows[g * part : (g + 1) * part, :] = dot(
             jnp.where(same, wide, jnp.zeros_like(wide)), table_v[g * span : (g + 1) * span, :]
         ).astype(BF16)
-    served[...] = dot(order[...], sorted_rows[...]).astype(BF16)
-    pl.semaphore_wait(barrier, dp_count + table_count - 2)
-    halves = [pl.ds(half * (unique // 2), unique // 2) for half in range(2)]
+    served[...] = dot(shift[...], sorted_rows[...]).astype(BF16)
     row_exchanges = [
         Exchange(
             "table", table_count, served.at[rows], rows_ref.at[rows], cap // 2, pair(row_sems.at[half])
@@ -414,9 +431,10 @@
     pick_exchange = Exchange("dp", dp_count, picks, picks_in, 2 * table_count, pair(pick_sems))
     pick_exchange.start()
 
-    marks[...] = halved(slot_ref[...], cap, unique)
-    prepare(marks, here, tall)
-    address_letters(fills_ref, dest_ref, marks, pick, chosen, flag)
+    for exchange in label_exchanges:
+        exchange.wait_recv()
+    prepare(slot_ref, labels_in, cap, here, tall, names, name_row)
+    address_letters(fills_ref, dest_ref, slot_ref, name_row, pick, chosen, flag)
     w_out_load.wait()
     aims_load.wait()
     weigh(fill_ref, length, w_out_ref, spread, dgated)
@@ -430,43 +448,62 @@
     attend(fill_ref, length, spread, dgated, normals, last)
     write_letters(rows_ref, w_out_ref, proj, last, pick, chosen, flag, message)
 
-    parts = grads.shape[0]
-    part_width = width // parts
+    pack = 2 * table_count
+    me = lax.axis_index("dp")
     letter_exchange = Exchange("dp", dp_count, message, letters, PACK, pair(letter_sems))
-    homes, totals = [], []
+    total_exchange = Exchange("dp", dp_count, ordered, arrived, pack, pair(total_sems))
+
+    def send_totals(half):
+        there = halves[half]
+        ordered[there, :] = dot(from_half(unique // 2, table_count), home[there, :]).astype(BF16)
+
+        def send(index, carry):
+            place = (me // 2 + index) % (dp_count // 2)
+            peer = 2 * place + half
+            source = ordered.at[
+                pl.ds(pl.multiple_of(half * (unique // 2) + place * pack, pack), pack)
+            ]
+            target = arrived.at[total_exchange.rows(me)]
+
+            @pl.when(peer != me)
+            def _():
+                pltpu.make_async_remote_copy(
+                    src_ref=source,
+                    dst_ref=target,
+                    send_sem=total_exchange.send,
+                    recv_sem=total_exchange.recv,
+                    device_id={"dp": peer},
+                ).start()
+
+            @pl.when(peer == me)
+            def _():
+                target[...] = source[...]
+
+            return carry
+
+        lax.fori_loop(0, dp_count // 2, send, 0)
+
+    homes = []
     for half, rows in enumerate(halves):
         finish(half, w_in_ref, gain_in_ref, tall, spread, slope, hat, inv, dproj, grads)
-        for p in range(parts):
-            home_exchange = Exchange(
-                "table", table_count, grads.at[p, rows], home.at[p, rows], cap // 2,
-                pair(home_sems.at[half, p]),
-            )
-            home_exchange.start()
-            homes.append(home_exchange)
+        home_exchange = Exchange(
+            "table", table_count, grads.at[rows], home.at[rows], cap // 2, pair(home_sems.at[half])
+        )
+        home_exchange.start()
+        homes.append(home_exchange)
         if half == 0:
             letter_exchange.start()
-    for p in range(parts):
-        homes[p].wait_recv()
-        homes[parts + p].wait_recv()
-        ordered[p, :, :] = dot(order[...], home[p, :, :], 0, 0).astype(BF16)
-        totals.append(
-            Exchange(
-                "dp", dp_count, ordered.at[p], arrived.at[p], 2 * table_count, pair(total_sems.at[p])
-            )
-        )
-        totals[p].start()
+    for half in range(2):
+        homes[half].wait_recv()
+        send_totals(half)
     letter_exchange.wait_recv()
     read_letters(letters, summary_ref)
     pick_exchange.wait_recv()
-    for exchange in row_exchanges + [pick_exchange, letter_exchange] + homes:
+    for exchange in label_exchanges + row_exchanges + [pick_exchange, letter_exchange] + homes:
         exchange.wait_send()
-    for p in range(parts):
-        totals[p].wait_recv()
-        total_ref[:, p * part_width : (p + 1) * part_width] = dot(
-            picks_in[...], arrived[p, :, :], 0, 0
-        )
-    for exchange in totals:
-        exchange.wait_send()
+    total_exchange.wait_recv()
+    total_ref[...] = dot(picks_in[...], arrived[...], 0, 0)
+    total_exchange.wait_send()
 
 
 def hand_on(summary_in, total_in, summary_out, total_out):
@@ -493,7 +530,6 @@
     work_count = block_count // 2
     events = block_count * length
     cols = w_in.shape[1]
-    parts, part_width = PARTS, width // PARTS
     dma = pltpu.SemaphoreType.DMA
     vmem = pltpu.VMEM
     fills = block_fill[0, 0]
@@ -519,23 +555,29 @@
         ]
         + compute_scratch(unique, events, cols, width, block_count, length)
         + [
-            vmem((block_count, length), jnp.int32),
+            vmem((unique, LANES), BF16),
+            vmem((unique, LANES), BF16),
+            vmem((unique, LANES), BF16),
+            vmem((unique, unique), BF16),
+            vmem((unique, LANES), jnp.int32),
+            vmem((8, unique), jnp.int32),
             vmem((block_count, unique), BF16),
             vmem((width // LANES, dp_count * PACK, block_count), BF16),
             vmem((dp_count * PACK, LANES), BF16),
             vmem((dp_count * PACK, LANES), BF16),
             vmem((dp_count * PACK, LANES), BF16),
-            vmem((parts, unique, part_width), BF16),
-            vmem((parts, unique, part_width), BF16),
-            vmem((parts, unique, part_width), BF16),
-            vmem((parts, unique, part_width), BF16),
+            vmem((unique, width), BF16),
+            vmem((unique, width), BF16),
+            vmem((unique, width), BF16),
+            vmem((unique, width), BF16),
             dma((max(1, dp_count // 8),)),
             dma((3,)),
             dma((2, 2)),
+            dma((2, 2)),
             dma((2,)),
             dma((2,)),
-            dma((2, parts, 2)),
-            dma((parts, 2)),
+            dma((2, 2)),
+            dma((2,)),
         ],
         compiler_params=pltpu.CompilerParams(
             vmem_limit_bytes=VMEM_BYTES, collective_id=0, has_side_effects=True

time: 65.7 us -> 65.7 us (level); the launches traced: 65.5 us -> 64.7 us
  Pallas kernels: 64.9 us -> 64.1 us
    pallas_call x1, Pallas kernels: 63.2 us -> 62.4 us  [body(): pl.pallas_call(functools.partial(step_kernel, dp_count), out_shape=(jax.S...]
where the time goes in v6:
time: 65.7 us; the launch traced here: 64.7 us
  Pallas kernels  64.1 us (98%)
    pallas_call x1, Pallas kernels, body(): pl.pallas_call(functools.partial(step_kernel, dp_count), out_shape=(jax.S...  62.4 us
    pallas_call x1, Pallas kernels, body(): pl.pallas_call(hand_on, out_shape=(jax.ShapeDtypeStruct((work_count, widt...  1.69 us

profile of v6, /device:TPU:1, one launch (start us, length us, event | category | flops | bytes accessed | tf_op | source)
XLA Modules:
  0.0 64.7 jit_solution(45133859622992924)
XLA Ops:
  0.6 62.4 %step.1 = (bf16[8,512]{1,0:T(8,128)(2,1)}, f32[128,512]{1,0:T(8,128)}) custom-call(s32[16]{0:T(128)} %bitcast.15, s32[8,64]{1,0:T(8,128)} %bitcast.12, s32[16,128]{1,0:T(8,128)} %bitcast.11, s32[1,16]{1,0:T(1,128)} %bitcast.16, s32[1,16]{1,0:T(1,128)} %bitcast.17, f32[1,512]{1,0:T(1,128)} %bitcast.13, f32[1,512]{1,0:T(1,128)} %bitcast.14, ...), custom_call_target="tpu_custom_call" | custom-call | tf_op jit(solution)/shard_map/step/pallas_call | solution.py:536
  63.0 1.7 %hand_on.1 = (bf16[8,512]{1,0:T(8,128)(2,1)}, f32[128,512]{1,0:T(8,128)}) custom-call(bf16[8,512]{1,0:T(8,128)(2,1)} %get-tuple-element.6.summary_in, f32[128,512]{1,0:T(8,128)} %get-tuple-element.7.total_in), custom_call_target="tpu_custom_call" | custom-call | tf_op jit(solution)/shard_map/hand_on/pallas_call | solution.py:591

commit v7 on v6

--- a/solution.py
+++ b/solution.py
@@ -17,7 +17,7 @@
 VMEM_BYTES = 60 * 1024 * 1024
 PROJECT_ROWS = 256
 GATHER_ROWS = 1024
-BLOCK_GROUP = 4
+BLOCK_GROUP = 8
 
 
 def dot(a, b, ca=1, cb=0):

time: 65.7 us -> 65.5 us (level)
  no operation moved by 1% of the time
where the time goes in v7:
time: 65.5 us; the launch traced here: 64.6 us
  Pallas kernels  64 us (98%)
    pallas_call x1, Pallas kernels, body(): pl.pallas_call(functools.partial(step_kernel, dp_count), out_shape=(jax.S...  62.3 us
    pallas_call x1, Pallas kernels, body(): pl.pallas_call(hand_on, out_shape=(jax.ShapeDtypeStruct((work_count, widt...  1.69 us

profile of v7, /device:TPU:1, one launch (start us, length us, event | category | flops | bytes accessed | tf_op | source)
XLA Modules:
  0.0 64.6 jit_solution(4131543898186963838)
XLA Ops:
  0.6 62.3 %step.1 = (bf16[8,512]{1,0:T(8,128)(2,1)}, f32[128,512]{1,0:T(8,128)}) custom-call(s32[16]{0:T(128)} %bitcast.15, s32[8,64]{1,0:T(8,128)} %bitcast.12, s32[16,128]{1,0:T(8,128)} %bitcast.11, s32[1,16]{1,0:T(1,128)} %bitcast.16, s32[1,16]{1,0:T(1,128)} %bitcast.17, f32[1,512]{1,0:T(1,128)} %bitcast.13, f32[1,512]{1,0:T(1,128)} %bitcast.14, ...), custom_call_target="tpu_custom_call" | custom-call | tf_op jit(solution)/shard_map/step/pallas_call | solution.py:536
  62.9 1.7 %hand_on.1 = (bf16[8,512]{1,0:T(8,128)(2,1)}, f32[128,512]{1,0:T(8,128)}) custom-call(bf16[8,512]{1,0:T(8,128)(2,1)} %get-tuple-element.6.summary_in, f32[128,512]{1,0:T(8,128)} %get-tuple-element.7.total_in), custom_call_target="tpu_custom_call" | custom-call | tf_op jit(solution)/shard_map/hand_on/pallas_call | solution.py:591
